TPU v7x, 128 devices: a whole 4x4x4 slice. The times are simulated.
128 devices in a mesh: seq: 16 (over z, x_lo, core), head: 4 (over y), cfg: 2 (over x_hi).
Axes of the slice: x: 4 (x_hi: 2, x_lo: 2; x = x_hi * 2 + x_lo), y: 4, z: 4, core: 2. Of those that a mesh axis runs over, the one named last changes fastest.
Arguments:
- query: bfloat16 [2, 4096, 1536], P('cfg', 'seq', 'head')
- key: bfloat16 [2, 4096, 1536], P('cfg', 'seq', 'head')
- value: bfloat16 [2, 4096, 1536], P('cfg', 'seq', 'head'), may hold values from -6 to 6
- cotangent: bfloat16 [4096, 3072], P('seq', ('head', 'cfg')), may hold values from -6 to 6
- key_block_slots: int32 [32, 16], P('seq'), may hold values from 0 to 31, as said below
- live_key_counts: int32 [32], P('seq'), may hold values from 1 to 16, as said below
- guidance_index: int32 [1], replicated, may hold values from 0 to 12
- output_weight_rows: bfloat16 [1536, 3072], P('head'), may hold values from -0.15625 to 0.15625
- lowering_matrix: bfloat16 [1536, 64], P('head'), may hold values from -0.15625 to 0.15625
- raising_matrix: bfloat16 [64, 3072], replicated, may hold values from -0.75 to 0.75
Outputs:
- grad_query: bfloat16 [2, 4096, 1536], P('cfg', 'seq', 'head')
- grad_key: bfloat16 [2, 4096, 1536], P('cfg', 'seq', 'head')
- grad_value: bfloat16 [2, 4096, 1536], P('cfg', 'seq', 'head')
- lowering_matrix_slope: float32 [1536, 64], P('head')
- grad_up: float32 [64, 3072], replicated
Inputs may be any that keep to these rules, and one draw needn't show every extreme that they name: `key_block_slots`: row i lists 16 different key blocks; slot 0 is block i itself. `live_key_counts`: query blocks of one index of seq share a density drawn for that index; some query block uses all 16 slots.
All inputs are finite; a program needn't handle non-finite values.
Results may differ from a plain program's by a relative error of at most 0.025.
Values may be sent and summed in bfloat16 or wider, within the bound.
A program may use at most 128 MiB of HBM per device.

v0:
```python
import jax
import jax.numpy as jnp
from jax import lax
from jax.sharding import PartitionSpec as P

HEAD_SIZE = 128
BLK = 128


def per_device(
    query,
    key,
    value,
    cotangent,
    key_block_slots,
    live_key_counts,
    guidance_index,
    output_weight_rows,
    lowering_matrix,
    raising_matrix,
):
    thirty_two_bit_real = jnp.float32
    truncated_sixteen_bit = jnp.bfloat16
    q_local = query[0]
    tok_rows, width = q_local.shape
    heads = width // HEAD_SIZE
    nblocks = tok_rows // BLK
    scale = HEAD_SIZE ** (-0.5)
    slots = jnp.arange(key_block_slots.shape[1], dtype=jnp.int32)
    weight = 1.5 + 0.5 * guidance_index[0].astype(thirty_two_bit_real)
    coef = jnp.where(lax.axis_index("cfg") == 0, weight, 1.0 - weight)
    grad_rows = lax.all_gather(cotangent, ("head", "cfg"), axis=1, tiled=True)
    output_gradient = (coef * grad_rows.astype(thirty_two_bit_real)).astype(truncated_sixteen_bit)
    keys_all, values_all = (
        lax.all_gather(key[0], "seq", axis=0, tiled=True),
        lax.all_gather(value[0], "seq", axis=0, tiled=True),
    )
    k_tiles = keys_all.reshape(-1, BLK, heads, HEAD_SIZE)
    v_tiles = values_all.reshape(-1, BLK, heads, HEAD_SIZE)
    q_tiles = q_local.reshape(nblocks, BLK, heads, HEAD_SIZE)

    def scores(i):
        ids = key_block_slots[i]
        live = slots < live_key_counts[i]
        s = (
            jnp.einsum(
                "qhd,jkhd->hqjk",
                q_tiles[i],
                k_tiles[ids],
                preferred_element_type=thirty_two_bit_real,
            )
            * scale
        )
        s = jnp.where(live[None, None, :, None], s, -jnp.inf)
        return (s, ids)

    def forward(i):
        s, ids = scores(i)
        top = jnp.max(s, axis=(2, 3), keepdims=True)
        lse = top + jnp.log(jnp.sum(jnp.exp(s - top), axis=(2, 3), keepdims=True))
        probs = jnp.exp(s - lse).astype(truncated_sixteen_bit)
        out = jnp.einsum(
            "hqjk,jkhd->qhd", probs, v_tiles[ids], preferred_element_type=thirty_two_bit_real
        ).astype(truncated_sixteen_bit)
        return (out, lse[:, :, 0, 0])

    o_tiles, lse = lax.map(forward, jnp.arange(nblocks, dtype=jnp.int32))
    merged_product_matrix = o_tiles.reshape(tok_rows, width)
    adapter_hidden_part = jnp.dot(
        merged_product_matrix, lowering_matrix, preferred_element_type=thirty_two_bit_real
    )
    low_rank = lax.psum(adapter_hidden_part, "head").astype(truncated_sixteen_bit)
    narrow_inner_slope = jnp.dot(
        output_gradient, raising_matrix.T, preferred_element_type=thirty_two_bit_real
    ).astype(truncated_sixteen_bit)
    d_o = (
        jnp.dot(output_gradient, output_weight_rows.T, preferred_element_type=thirty_two_bit_real)
        + jnp.dot(narrow_inner_slope, lowering_matrix.T, preferred_element_type=thirty_two_bit_real)
    ).astype(truncated_sixteen_bit)
    lowering_product = jnp.dot(
        merged_product_matrix.T, narrow_inner_slope, preferred_element_type=thirty_two_bit_real
    )
    up_part = jnp.dot(low_rank.T, output_gradient, preferred_element_type=thirty_two_bit_real)
    lowering_matrix_slope, grad_up = (
        lax.psum(lowering_product.astype(jnp.bfloat16), ("seq", "cfg")).astype(jnp.float32),
        lax.psum(up_part.astype(jnp.bfloat16), ("seq", "cfg")).astype(jnp.float32),
    )
    do_tiles = d_o.reshape(nblocks, BLK, heads, HEAD_SIZE)
    delta = jnp.sum(
        do_tiles.astype(thirty_two_bit_real) * o_tiles.astype(thirty_two_bit_real), axis=3
    )

    def query_side(carry, i):
        dk_acc, dv_acc = carry
        s, ids = scores(i)
        probs = jnp.exp(s - lse[i][:, :, None, None])
        pb = probs.astype(truncated_sixteen_bit)
        dp = jnp.einsum(
            "qhd,jkhd->hqjk", do_tiles[i], v_tiles[ids], preferred_element_type=thirty_two_bit_real
        )
        ds = (probs * (dp - jnp.transpose(delta[i])[:, :, None, None])).astype(
            truncated_sixteen_bit
        )
        dq = (
            jnp.einsum(
                "hqjk,jkhd->qhd", ds, k_tiles[ids], preferred_element_type=thirty_two_bit_real
            )
            * scale
        ).astype(truncated_sixteen_bit)
        dk_acc = dk_acc.at[ids].add(
            jnp.einsum("hqjk,qhd->jkhd", ds, q_tiles[i], preferred_element_type=thirty_two_bit_real)
            * scale
        )
        dv_acc = dv_acc.at[ids].add(
            jnp.einsum(
                "hqjk,qhd->jkhd", pb, do_tiles[i], preferred_element_type=thirty_two_bit_real
            )
        )
        return ((dk_acc, dv_acc), dq)

    zeros = jnp.zeros(k_tiles.shape, thirty_two_bit_real)
    (dk_acc, dv_acc), dq = lax.scan(
        query_side, (zeros, zeros), jnp.arange(nblocks, dtype=jnp.int32)
    )
    total = k_tiles.shape[0] * BLK
    dk_sum, dv_sum = (
        lax.psum_scatter(dk_acc.reshape(total, width), "seq", scatter_dimension=0, tiled=True),
        lax.psum_scatter(dv_acc.reshape(total, width), "seq", scatter_dimension=0, tiled=True),
    )
    grad_k = dk_sum.astype(truncated_sixteen_bit)
    grad_v = dv_sum.astype(truncated_sixteen_bit)
    grad_q = dq.reshape(tok_rows, width)
    return (grad_q[None], grad_k[None], grad_v[None], lowering_matrix_slope, grad_up)


def solution(mesh):
    in_specs = (
        P("cfg", "seq", "head"),
        P("cfg", "seq", "head"),
        P("cfg", "seq", "head"),
        P("seq", ("head", "cfg")),
        P("seq", None),
        P("seq"),
        P(),
        P("head", None),
        P("head", None),
        P(),
    )
    out_specs = (
        P("cfg", "seq", "head"),
        P("cfg", "seq", "head"),
        P("cfg", "seq", "head"),
        P("head", None),
        P(),
    )
    return jax.shard_map(
        per_device, mesh=mesh, in_specs=in_specs, out_specs=out_specs, check_vma=False
    )
```

profile of v0, /device:TPU:0, one launch (start us, length us, event | category | flops | bytes accessed | tf_op | source)
XLA Modules:
  0.0 492.3 jit_solution(11893687253525760228)
XLA Ops:
  10.1 1.0 reshape.204
  11.2 51.3 %all-gather.6.cloned.1.call-done = bf16[256,3072]{1,0:T(8,128)(2,1)} async-done(((bf16[256,384]{1,0:T(8,128)(2,1)}), bf16[256,3072]{1,0:T(8,128)(2,1)}) %all-gather.6.cloned.1.call-update) | async-done | bytes 1572880 | tf_op jit(solution)/shard_map/all_gather | solution.py:32
  62.4 2.1 fusion.62
  64.5 2.4 fusion.60
  67.6 30.5 %all-gather.10.cloned.1.call-done = bf16[1,4096,384]{2,1,0:T(8,128)(2,1)} async-done(((bf16[1,256,384]{2,1,0:T(8,128)(2,1)}), bf16[1,4096,384]{2,1,0:T(8,128)(2,1)}) %all-gather.10.cloned.1.call-update) | async-done | bytes 3145744 | tf_op jit(solution)/shard_map/all_gather | solution.py:36
  98.2 9.0 %reshape.206 = bf16[32,128,3,128]{3,2,1,0:T(4,128)(2,1)} reshape(bf16[1,4096,384]{2,1,0:T(8,128)(2,1)} %all-gather.10.cloned.1.call-done) | data formatting | bytes 6291456 | tf_op jit(solution)/shard_map/reshape | solution.py:39
  107.2 28.7 %all-gather.8.cloned.1.call-done = bf16[1,4096,384]{2,1,0:T(8,128)(2,1)} async-done(((bf16[1,256,384]{2,1,0:T(8,128)(2,1)}), bf16[1,4096,384]{2,1,0:T(8,128)(2,1)}) %all-gather.8.cloned.1.call-update) | async-done | bytes 3145744 | tf_op jit(solution)/shard_map/all_gather | solution.py:35
  135.9 9.0 %reshape.205 = bf16[32,128,3,128]{3,2,1,0:T(4,128)(2,1)} reshape(bf16[1,4096,384]{2,1,0:T(8,128)(2,1)} %all-gather.8.cloned.1.call-done) | data formatting | bytes 6291456 | tf_op jit(solution)/shard_map/reshape | solution.py:38
  144.9 37.4 %while.28 = (s32[]{:T(128)}, bf16[2,128,3,128]{1,3,2,0:T(8,128)(2,1)S(1)}, f32[2,3,128]{2,1,0:T(4,128)S(1)}, s32[2]{0:T(128)S(1)}, s32[2,16]{1,0:T(2,128)}, /*in...) while((s32[]{:T(128)}, ...), condition=%wide.region_3.4_spmd.clone, body=%wide.region_0.3_spmd.clone.sunk | while | flops 411353792 | bytes 29053000 | solution.py:67
  147.4 1.2 dynamic_slice.101
  150.0 5.8 %gather_fusion.1 = bf16[16,128,3,128]{3,2,1,0:T(4,128)(2,1)} fusion(bf16[32,128,3,128]{3,2,1,0:T(4,128)(2,1)} %get-tuple-element.471, s32[1024]{0:T(1024)S(1)} %pad_clamp_fusion.4), kind=kCustom, calls=%fused_computation.clone.clone.1 | custom fusion | bytes 3145792 | tf_op jit(solution)/shard_map/while/body/eval_jaxpr/gather | solution.py:63
  155.8 4.5 gather_fusion
  162.4 1.2 fusion.103
  166.1 1.2 dynamic_slice.101
  168.7 5.8 %gather_fusion.1 = bf16[16,128,3,128]{3,2,1,0:T(4,128)(2,1)} fusion(bf16[32,128,3,128]{3,2,1,0:T(4,128)(2,1)} %get-tuple-element.471, s32[1024]{0:T(1024)S(1)} %pad_clamp_fusion.4), kind=kCustom, calls=%fused_computation.clone.clone.1 | custom fusion | bytes 3145792 | tf_op jit(solution)/shard_map/while/body/eval_jaxpr/gather | solution.py:63
  174.5 4.5 gather_fusion
  180.1 0.7 exponential_reduce_fusion.2
  181.0 1.2 fusion.103
  182.9 17.5 %psum.22 = bf16[256,64]{0,1:T(8,128)(2,1)S(1)} all-reduce(f32[256,64]{0,1:T(8,128)S(1)} %fusion.63), channel_id=1, replica_groups=mesh['seq'=16,'head'=4,'cfg'=2] {'head'}, use_global_device_ids=true, to_apply=%region_12.13 | all-reduce | flops 16384 | bytes 98304 | tf_op jit(solution)/shard_map/psum | solution.py:72
  200.5 2.6 convolution_convert_fusion
  203.6 0.7 broadcast.67
  204.3 3.4 broadcast_in_dim.53.clone
  207.7 3.4 broadcast_in_dim.53
  211.2 94.9 %while.29 = (s32[]{:T(128)}, f32[32,128,3,128]{3,1,2,0:T(8,128)}, f32[32,128,3,128]{3,1,2,0:T(8,128)}, bf16[2,128,3,128]{1,3,2,0:T(8,128)(2,1)}, s32[2]{0:T(128)...) while((s32[]{:T(128)}, f32[32,128,3,128]{3,1,2,0:T(8,128)}, ...), condition=%wide.region_8.9_spmd.clone, body=%wide.region_5.8_spmd.clone.sunk | while | flops 1016955968 | bytes 92263512 | solution.py:122
  213.6 1.2 dynamic_slice.110
  216.3 5.8 %gather_fusion.3 = bf16[16,128,3,128]{3,2,1,0:T(4,128)(2,1)} fusion(bf16[32,128,3,128]{3,2,1,0:T(4,128)(2,1)} %get-tuple-element.521, s32[1024]{0:T(1024)S(1)} %pad_clamp_fusion.5), kind=kCustom, calls=%fused_computation.3.clone.clone.1 | custom fusion | bytes 3145792 | tf_op jit(solution)/shard_map/while/body/eval_jaxpr/gather | solution.py:99
  222.0 5.8 %gather_fusion.2 = bf16[16,128,3,128]{3,2,1,0:T(4,128)(2,1)} fusion(bf16[32,128,3,128]{3,2,1,0:T(4,128)(2,1)} %get-tuple-element.518, s32[1024]{0:T(1024)S(1)} %pad_clamp_fusion.5), kind=kCustom, calls=%fused_computation.2.clone.clone.1 | custom fusion | bytes 3145792 | tf_op jit(solution)/shard_map/while/body/eval_jaxpr/gather | solution.py:49
  227.8 3.0 copy.147
  231.4 1.0 copy-done.5
  232.4 1.3 multiply_convert_fusion.8
  233.7 1.3 fusion.116
  235.0 0.9 convolution_bitcast_fusion.3
  235.9 2.4 copy.150
  238.3 2.0 multiply_bitcast_fusion.2
  240.3 2.4 copy.149
  242.7 8.7 %scatter_fusion = f32[32,128,3,128]{3,1,2,0:T(8,128)} fusion(f32[32,128,3,128]{3,1,2,0:T(8,128)} %get-tuple-element.495, s32[16]{0:T(128)S(1)} %fusion.114, f32[16,128,3,128]{3,1,2,0:T(8,128)} %copy.149), kind=kCustom, calls=%fused_computation.4.clone.clone.1 | custom fusion | flops 786432 | bytes 9437248 | tf_op jit(solution)/shard_map/while/body/eval_jaxpr/scatter-add | solution.py:110
  251.4 7.3 %scatter_fusion.1 = f32[32,128,3,128]{3,1,2,0:T(8,128)} fusion(f32[32,128,3,128]{3,1,2,0:T(8,128)} %get-tuple-element.496, s32[16]{0:T(128)S(1)} %fusion.114, f32[16,128,3,128]{3,1,2,0:T(8,128)S(1)} %copy-done.2), kind=kCustom, calls=%fused_computation.5.clone.clone.1 | custom fusion | flops 786432 | bytes 9437248 | tf_op jit(solution)/shard_map/while/body/eval_jaxpr/scatter-add | solution.py:114
  261.1 1.2 dynamic_slice.110
  263.8 5.7 %gather_fusion.3 = bf16[16,128,3,128]{3,2,1,0:T(4,128)(2,1)} fusion(bf16[32,128,3,128]{3,2,1,0:T(4,128)(2,1)} %get-tuple-element.521, s32[1024]{0:T(1024)S(1)} %pad_clamp_fusion.5), kind=kCustom, calls=%fused_computation.3.clone.clone.1 | custom fusion | bytes 3145792 | tf_op jit(solution)/shard_map/while/body/eval_jaxpr/gather | solution.py:99
  269.5 5.8 %gather_fusion.2 = bf16[16,128,3,128]{3,2,1,0:T(4,128)(2,1)} fusion(bf16[32,128,3,128]{3,2,1,0:T(4,128)(2,1)} %get-tuple-element.518, s32[1024]{0:T(1024)S(1)} %pad_clamp_fusion.5), kind=kCustom, calls=%fused_computation.2.clone.clone.1 | custom fusion | bytes 3145792 | tf_op jit(solution)/shard_map/while/body/eval_jaxpr/gather | solution.py:49
  275.3 3.0 copy.147
  278.9 1.0 copy-done.5
  279.9 1.3 multiply_convert_fusion.8
  281.2 1.3 fusion.116
  282.4 0.9 convolution_bitcast_fusion.3
  283.4 2.4 copy.150
  285.7 2.0 multiply_bitcast_fusion.2
  287.8 2.4 copy.149
  290.2 8.6 %scatter_fusion = f32[32,128,3,128]{3,1,2,0:T(8,128)} fusion(f32[32,128,3,128]{3,1,2,0:T(8,128)} %get-tuple-element.495, s32[16]{0:T(128)S(1)} %fusion.114, f32[16,128,3,128]{3,1,2,0:T(8,128)} %copy.149), kind=kCustom, calls=%fused_computation.4.clone.clone.1 | custom fusion | flops 786432 | bytes 9437248 | tf_op jit(solution)/shard_map/while/body/eval_jaxpr/scatter-add | solution.py:110
  298.8 7.3 %scatter_fusion.1 = f32[32,128,3,128]{3,1,2,0:T(8,128)} fusion(f32[32,128,3,128]{3,1,2,0:T(8,128)} %get-tuple-element.496, s32[16]{0:T(128)S(1)} %fusion.114, f32[16,128,3,128]{3,1,2,0:T(8,128)S(1)} %copy-done.2), kind=kCustom, calls=%fused_computation.5.clone.clone.1 | custom fusion | flops 786432 | bytes 9437248 | tf_op jit(solution)/shard_map/while/body/eval_jaxpr/scatter-add | solution.py:114
  306.1 6.8 %copy.83 = f32[32,128,3,128]{1,0,3,2:T(8,128)} copy(f32[32,128,3,128]{3,1,2,0:T(8,128)} %get-tuple-element.135) | data formatting | bytes 12582912 | tf_op jit(solution)/shard_map/while | solution.py:122
  313.0 11.4 %copy.136 = f32[48,8,32,128]{3,1,2,0:T(8,128)} copy(f32[48,8,32,128]{3,2,1,0:T(8,128)} %bitcast.217) | data formatting | bytes 12582912
  324.4 6.9 %copy.84 = f32[32,128,3,128]{1,0,3,2:T(8,128)} copy(f32[32,128,3,128]{3,1,2,0:T(8,128)} %get-tuple-element.136) | data formatting | bytes 12582912 | tf_op jit(solution)/shard_map/while | solution.py:122
  331.3 11.5 %copy.135 = f32[48,8,32,128]{3,1,2,0:T(8,128)} copy(f32[48,8,32,128]{3,2,1,0:T(8,128)} %bitcast.218) | data formatting | bytes 12582912
  342.8 0.9 copy-done.7
  343.9 127.3 %psum.21 = bf16[384,64]{0,1:T(8,128)(2,1)S(1)} all-reduce(bf16[384,64]{0,1:T(8,128)(2,1)S(1)} %convolution_convert_fusion.1), channel_id=1, replica_groups=mesh['seq'=16,'head'=4,'cfg'=2] {'seq','cfg'}, use_global_device_ids=true, to_apply=%region_11.12 | all-reduce | flops 24576 | bytes 98304 | tf_op jit(solution)/shard_map/psum | solution.py:85
  471.9 1.1 copy.96
  473.0 0.9 reshape.203
  473.9 1.9 convert_element_type.77
  475.8 1.0 convert_bitcast_fusion.1
  476.8 0.8 copy.87
  477.6 5.8 %reduce-scatter.5.cloned.1.call-done = f32[256,384]{0,1:T(8,128)} async-done(((f32[4096,384]{0,1:T(8,128)}), f32[256,384]{0,1:T(8,128)}) %reduce-scatter.5.cloned.1.call-update) | async-done | bytes 393232 | tf_op jit(solution)/shard_map/reduce_scatter | solution.py:128
  483.4 1.0 convert_bitcast_fusion
  484.4 0.8 copy.88
  (102 shorter events, 17.2 us)
Async XLA Ops:
  7.2 57.3 %copy-start = (bf16[384,3072]{1,0:T(8,128)(2,1)S(1)}, bf16[384,3072]{1,0:T(8,128)(2,1)}, u32[]{:S(2)}) copy-start(bf16[384,3072]{1,0:T(8,128)(2,1)} %param.21) | copy-start | bytes 7077892
  7.2 55.2 %all-gather.6.cloned.1.call-start = ((), (), s32[]{:S(2)}) async-start(), calls=%async_computation.2 | async-start | bytes 1769472 | tf_op jit(solution)/shard_map/all_gather | solution.py:32
  7.9 90.2 %all-gather.10.cloned.1.call-start = ((), (), s32[]{:S(2)}) async-start(), calls=%async_computation.7 | async-start | bytes 3342336 | tf_op jit(solution)/shard_map/all_gather | solution.py:36
  8.7 127.2 %all-gather.8.cloned.1.call-start = ((), (), s32[]{:S(2)}) async-start(), calls=%async_computation.6 | async-start | bytes 3342336 | tf_op jit(solution)/shard_map/all_gather | solution.py:35
  9.4 464.5 %all-reduce.2.cloned.1.call-start = ((), (), s32[]{:S(2)}) async-start(), calls=%async_computation.5 | async-start | bytes 786432 | tf_op jit(solution)/shard_map/psum | solution.py:86
  64.5 2.5 copy-start.9
  64.5 2.5 copy-start.8
  160.8 1.6 copy-start.4
  179.4 1.6 copy-start.4
  182.8 25.0 %copy-start.6 = (bf16[2,128,3,128]{1,0,3,2:T(2,128)(2,1)}, bf16[2,128,3,128]{1,0,3,2:T(2,128)(2,1)S(1)}, u32[]{:S(2)}) copy-start(bf16[2,128,3,128]{1,0,3,2:T(2,128)(2,1)S(1)} %copy.76) | copy-start | bytes 589828
  203.1 272.7 %reduce-scatter.3.cloned.1.call-start = ((), (), s32[]{:S(2)}) async-start(), calls=%async_computation.3 | async-start | bytes 6684672 | tf_op jit(solution)/shard_map/reduce_scatter | solution.py:127
  211.2 5.0 %copy-start.13 = (s32[2]{0:T(128)}, s32[2]{0:T(128)S(1)}, u32[]{:S(2)}) copy-start(s32[2]{0:T(128)S(1)} %get-tuple-element.514) | copy-start | bytes 28 | tf_op jit(solution)/shard_map/while
  215.5 15.9 %copy-start.11 = (pred[16]{0:T(512)(128)(4,1)}, pred[16]{0:T(512)(128)(4,1)S(1)}, u32[]{:S(2)}) copy-start(pred[16]{0:T(512)(128)(4,1)S(1)} %iota_compare_fusion.5) | copy-start | bytes 52 | tf_op jit(solution)/shard_map/while
  230.8 1.6 copy-start.5
  233.7 1.3 copy-start.3
  233.7 1.3 copy-start.12
  242.7 8.7 %copy-start.2 = (f32[16,128,3,128]{3,1,2,0:T(8,128)S(1)}, f32[16,128,3,128]{3,1,2,0:T(8,128)}, u32[]{:S(2)}) copy-start(f32[16,128,3,128]{3,1,2,0:T(8,128)} %copy.150) | copy-start | bytes 9437188 | tf_op jit(solution)/shard_map/while
  251.4 7.3 %copy-start.14 = (s32[2]{0:T(128)S(1)}, s32[2]{0:T(128)}, u32[]{:S(2)}) copy-start(s32[2]{0:T(128)} %copy-done.13) | copy-start | bytes 28 | tf_op jit(solution)/shard_map/while
  258.7 5.0 %copy-start.13 = (s32[2]{0:T(128)}, s32[2]{0:T(128)S(1)}, u32[]{:S(2)}) copy-start(s32[2]{0:T(128)S(1)} %get-tuple-element.514) | copy-start | bytes 28 | tf_op jit(solution)/shard_map/while
  263.0 15.9 %copy-start.11 = (pred[16]{0:T(512)(128)(4,1)}, pred[16]{0:T(512)(128)(4,1)S(1)}, u32[]{:S(2)}) copy-start(pred[16]{0:T(512)(128)(4,1)S(1)} %iota_compare_fusion.5) | copy-start | bytes 52 | tf_op jit(solution)/shard_map/while
  278.3 1.6 copy-start.5
  281.2 1.3 copy-start.3
  281.2 1.3 copy-start.12
  290.2 8.7 %copy-start.2 = (f32[16,128,3,128]{3,1,2,0:T(8,128)S(1)}, f32[16,128,3,128]{3,1,2,0:T(8,128)}, u32[]{:S(2)}) copy-start(f32[16,128,3,128]{3,1,2,0:T(8,128)} %copy.150) | copy-start | bytes 9437188 | tf_op jit(solution)/shard_map/while
  298.8 7.3 %copy-start.14 = (s32[2]{0:T(128)S(1)}, s32[2]{0:T(128)}, u32[]{:S(2)}) copy-start(s32[2]{0:T(128)} %copy-done.13) | copy-start | bytes 28 | tf_op jit(solution)/shard_map/while
  324.4 159.0 %reduce-scatter.5.cloned.1.call-start = ((), (), s32[]{:S(2)}) async-start(), calls=%async_computation.4 | async-start | bytes 6684672 | tf_op jit(solution)/shard_map/reduce_scatter | solution.py:128
  342.8 0.9 copy-start.7
  342.8 0.9 copy-start.10
  343.7 141.5 %copy-start.1 = (bf16[384,3072]{1,0:T(8,128)(2,1)S(1)}, bf16[384,3072]{1,0:T(8,128)(2,1)}, u32[]{:S(2)}) copy-start(bf16[384,3072]{1,0:T(8,128)(2,1)} %param.21) | copy-start | bytes 7077892
Sparse Core Ops, SparseCore 0:
  10.2 52.1 all-gather.5
  64.1 33.9 all-gather.9
  99.9 35.9 all-gather.7
  203.2 101.1 all-reduce.1
  324.5 77.7 reduce-scatter.2
  404.5 78.8 reduce-scatter.4
where the time goes:
time: 502 us; the launch traced here: 492 us
  blocking collectives  145 us (29%)
  local copies, waits for them, and re-layouts  138 us (27%)
  waiting for transfers between devices  118 us (24%)
  other arithmetic  43.6 us (9%)
  matrix products  23.4 us (5%)
  between operations  15.2 us (3%)
  loops' own time  7.93 us (2%)
    psum x1, blocking collectives, per_device(): lax.psum(lowering_product.astype(jnp.bfloat16), ('seq', 'cfg'))  127 us
    all_gather x1, waiting for transfers between devices, per_device(): grad_rows = lax.all_gather(cotangent, ('head', 'cfg'), axis=1, tiled=True)  51.3 us
    all_gather x1, waiting for transfers between devices, per_device(): lax.all_gather(value[0], 'seq', axis=0, tiled=True)  30.5 us
    all_gather x1, waiting for transfers between devices, per_device(): lax.all_gather(key[0], 'seq', axis=0, tiled=True)  28.7 us
    unnamed x22, local copies, waits for them, and re-layouts  27.6 us
    gather x8, local copies, waits for them, and re-layouts, scores(): k_tiles[ids]  27.5 us
    psum x1, blocking collectives, per_device(): lax.psum(adapter_hidden_part, 'head').astype(truncated_sixteen_bit)  17.5 us
    scatter-add x2, other arithmetic, query_side(): dk_acc.at[ids]  17.3 us
  transfers between devices with their start and end apart: 6, of which 4 were waited for; matrix products, arithmetic and copies ran while one was open for 31% of the time, Pallas kernels for 0%

commit v1 on v0

v1 whole, which is shorter than its diff:
```python
import functools
import math

import jax
import jax.numpy as jnp
from jax import lax
from jax.experimental import pallas as pl
from jax.experimental.pallas import tpu as pltpu
from jax.sharding import PartitionSpec as P

HD = 128
NH = 3
W = 384
T = 256
NK = 1024
RANK = 64
SCALE = HD ** -0.5
C2 = SCALE * math.log2(math.e)
BIG = 3.0e38
F32 = jnp.float32
BF16 = jnp.bfloat16
MESH = pl.DeviceIdType.MESH
NSEM = 96


def nn(a, b):
    return lax.dot_general(a, b, (((1,), (0,)), ((), ())), preferred_element_type=F32)


def nt(a, b):
    return lax.dot_general(a, b, (((1,), (1,)), ((), ())), preferred_element_type=F32)


def kernel(
    q_in, k_in, v_in, cot_in, w_in, low_in, up_in, slots_ref, counts_ref, guide_ref,
    dq_out, dk_out, dv_out, slope_out, gup_out,
    Q, K, V, KT, VT, COT, WB, LOW, PART, PARTR, DOT, BIAS, PR, OT, STO, STR,
    DK, DV, DQB, DQR, DKB, DVB, DKR, DVR, DKX, DVX, DKXR, DVXR,
    LHB, LHR, LHY, LHYR, LHC, LHCR, GSB, GSR, S1B, S1R, S2B, S2R, GU, SL, SLT,
    send_sem, recv_sem, loc_sem,
):
    s, hy, c = lax.axis_index("seq"), lax.axis_index("head"), lax.axis_index("cfg")
    z, x, kc = s // 4, (s // 2) % 2, s % 2
    g = s % 4
    peer = {}
    for d in (1, 2, 3):
        peer["z%d" % d] = {"seq": ((z + d) % 4) * 4 + g}
        peer["y%d" % d] = {"head": (hy + d) % 4}
    peer["sib"] = {"seq": z * 4 + x * 2 + (1 - kc)}
    peer["x"] = {"seq": z * 4 + (1 - x) * 2 + kc}
    peer["xo"] = {"seq": z * 4 + (1 - x) * 2 + (1 - kc)}
    peer["cfg"] = {"cfg": 1 - c}

    count = [0, 0]
    started = []

    def local(src, dst):
        cp = pltpu.make_async_copy(src, dst, loc_sem.at[count[1]])
        count[1] += 1
        cp.start()
        return cp

    def send(src, dst, to):
        i = count[0]
        count[0] += 1
        cp = pltpu.make_async_remote_copy(
            src_ref=src, dst_ref=dst, send_sem=send_sem.at[i], recv_sem=recv_sem.at[i],
            device_id=peer[to], device_id_type=MESH,
        )
        cp.start()
        started.append(cp)
        return cp

    def ring(axis, src, dst):
        got = {}
        for d in (1, 3, 2):
            e = (4 - d) % 4
            got[e] = send(src(d), dst(e), "%s%d" % (axis, d))
        return got

    l_cot = local(cot_in, COT.at[0])
    l_w = []
    for j in range(4):
        col = pl.multiple_of((((hy + j) % 4) * 2 + c) * W, 128)
        l_w.append(local(w_in.at[:, pl.ds(col, W)], WB.at[j, pl.ds(0, W)]))
        l_w.append(local(up_in.at[:, pl.ds(col, W)], WB.at[j, pl.ds(W, RANK)]))
    l_kv = [local(k_in, K.at[pl.ds(0, T)]), local(v_in, V.at[pl.ds(0, T)])]
    l_q = local(q_in, Q.at[pl.ds(0, T)])
    l_low = local(low_in, LOW)

    barrier = pltpu.get_barrier_semaphore()
    for name in peer:
        pl.semaphore_signal(barrier, inc=1, device_id=peer[name], device_id_type=MESH)
    pl.semaphore_wait(barrier, len(peer))

    r_cot = ring("y", lambda d: cot_in, lambda e: COT.at[e])
    r_k = {}
    r_v = {}
    for to, r in (("x", 2), ("sib", 1)):
        r_k[r] = send(k_in, K.at[pl.ds(r * T, T)], to)
        r_v[r] = send(v_in, V.at[pl.ds(r * T, T)], to)
    r_q = ring("z", lambda d: q_in, lambda e: Q.at[pl.ds(e * T, T)])

    row = lax.broadcasted_iota(jnp.int32, (8, T), 0)
    lane = lax.broadcasted_iota(jnp.int32, (8, T), 1)
    rx, rk = row // 4, (row // 2) % 2
    gx = x + rx - 2 * x * rx
    gk = kc + rk - 2 * kc * rk
    base_block = 2 * (gx * 2 + gk) + row % 2
    for d in range(4):
        block = base_block + 8 * ((z + d) % 4)
        live = jnp.zeros((8, T), F32)
        for qb in range(2):
            n = counts_ref[qb]
            for j in range(16):
                want = jnp.where(j < n, slots_ref[qb, j], -1)
                hit = jnp.logical_and(block == want, lane // 128 == qb)
                live = jnp.where(hit, 1.0, live)
        BIAS[d] = jnp.where(live > 0, BIG, -BIG)
    r_bias = ring("z", lambda d: BIAS.at[d], lambda e: BIAS.at[4 + e])

    weight = 1.5 + 0.5 * guide_ref[0].astype(F32)
    coef = jnp.where(c == 0, weight, 1.0 - weight)

    l_cot.wait()
    for cp in l_w:
        cp.wait()
    acc = nt(WB[0], COT[0])
    for e in (1, 3, 2):
        r_cot[e].wait_recv()
        acc += nt(WB[e], COT[e])
    PART[...] = acc.astype(BF16)
    r_part = send(PART, PARTR, "cfg")

    r_k[2].wait_recv()
    r_k[3] = send(K.at[pl.ds(2 * T, T)], K.at[pl.ds(3 * T, T)], "sib")
    r_v[2].wait_recv()
    r_v[3] = send(V.at[pl.ds(2 * T, T)], V.at[pl.ds(3 * T, T)], "sib")

    l_low.wait()
    r_part.wait_recv()
    base = (PART[...].astype(F32) + PARTR[...].astype(F32)) * coef
    dlh = base[W:].astype(BF16)
    DOT[0, W:] = dlh
    DOT[0, :W] = (base[:W] + nn(LOW[...], dlh)).astype(BF16)
    r_do = ring("z", lambda d: DOT.at[0], lambda e: DOT.at[e])

    for cp in l_kv:
        cp.wait()
    for r in (1, 3):
        r_k[r].wait_recv()
        r_v[r].wait_recv()
    for h in range(NH):
        hs = slice(h * HD, (h + 1) * HD)
        KT[h] = K[:, hs].T
        VT[h] = V[:, hs].T

    l_q.wait()
    m2 = {}
    for d in (0, 1, 3, 2):
        if d:
            r_q[d].wait_recv()
            r_bias[d].wait_recv()
        bias = BIAS[4 + d] if d else BIAS[0]
        for h in range(NH):
            hs = slice(h * HD, (h + 1) * HD)
            sc = nt(K[:, hs], Q[d * T:(d + 1) * T, hs])
            sc = jnp.minimum(sc.reshape(8, 128, T), bias[:, None, :]).reshape(NK, T)
            top = jnp.max(sc, axis=0, keepdims=True) * C2
            p = jnp.exp2(sc * C2 - top)
            total = jnp.sum(p, axis=0, keepdims=True)
            pb = p.astype(BF16)
            PR[h, :, d * T:(d + 1) * T] = pb
            OT[h, d] = nn(VT[h], pb) / total
            STO[d, h:h + 1] = top + jnp.log2(total)
            m2[h, d] = top

    for d in (0, 1, 3, 2):
        if d:
            r_do[d].wait_recv()
        for h in range(NH):
            do = DOT[d, h * HD:(h + 1) * HD].astype(F32)
            STO[d, 3 + h:4 + h] = jnp.sum(do * OT[h, d], axis=0, keepdims=True)
        STO[d, 6:8] = jnp.zeros((2, T), F32)
    r_st = ring("z", lambda d: STO, lambda e: STR.at[e - 1])
    for e in (1, 3, 2):
        r_st[e].wait_recv()

    fac, delta = {}, {}
    slope = [jnp.zeros((RANK, HD), F32) for _ in range(NH)]
    for d in range(4):
        lh = jnp.zeros((RANK, T), F32)
        for h in range(NH):
            parts = [STO[d, h:h + 1]] + [STR[e - 1, (d - e) % 4, h:h + 1] for e in (1, 2, 3)]
            dels = [STO[d, 3 + h:4 + h]] + [STR[e - 1, (d - e) % 4, 3 + h:4 + h] for e in (1, 2, 3)]
            top = functools.reduce(jnp.maximum, parts)
            ws = [jnp.exp2(p - top) for p in parts]
            total = ws[0] + ws[1] + ws[2] + ws[3]
            fac[h, d] = jnp.exp2(m2[h, d] - top) / total
            delta[h, d] = (ws[0] * dels[0] + ws[1] * dels[1] + ws[2] * dels[2] + ws[3] * dels[3]) / total
            ob = (OT[h, d] * (ws[0] / total)).astype(BF16)
            low = LOW[h * HD:(h + 1) * HD]
            lh += lax.dot_general(low, ob, (((0,), (0,)), ((), ())), preferred_element_type=F32)
            slope[h] += nt(DOT[d, W:], ob)
        LHB[d] = (lh * coef).astype(BF16)
    r_lh = ring("z", lambda d: LHB.at[d], lambda e: LHR.at[e - 1])

    def attention_back(h):
        hs = slice(h * HD, (h + 1) * HD)
        dk = jnp.zeros((NK, HD), F32)
        dv = jnp.zeros((NK, HD), F32)
        for d in range(4):
            do = DOT[d, hs]
            dp = nn(V[:, hs], do)
            p = PR[h, :, d * T:(d + 1) * T].astype(F32) * fac[h, d]
            ds = (p * (dp - delta[h, d])).astype(BF16)
            dk += nn(ds, Q[d * T:(d + 1) * T, hs])
            dv += nt(p.astype(BF16), do)
            dq = nn(KT[h], ds) * SCALE
            DQB[h, d] = dq.astype(BF16)
            if d == 0:
                DQ0[h] = dq
        DK[h] = dk * SCALE
        DV[h] = dv
        DKB[h] = DK[h].astype(BF16)
        DVB[h] = dv.astype(BF16)
        r_dq[h] = ring("z", lambda d: DQB.at[h, d], lambda e: DQR.at[h, e - 1])
        for r in (3, 1):
            rows = pl.ds(r * T, T)
            i = 0 if r == 3 else 1
            r_dks[h, r] = send(DKB.at[h, rows], DKR.at[h, i], "sib")
            r_dvs[h, r] = send(DVB.at[h, rows], DVR.at[h, i], "sib")

    def cross(h):
        rows = slice(2 * T, 3 * T)
        r_dks[h, 3].wait_recv()
        DKX[h] = (DK[h, rows] + DKR[h, 0].astype(F32)).astype(BF16)
        r_dkx[h] = send(DKX.at[h], DKXR.at[h], "x")
        r_dvs[h, 3].wait_recv()
        DVX[h] = (DV[h, rows] + DVR[h, 0].astype(F32)).astype(BF16)
        r_dvx[h] = send(DVX.at[h], DVXR.at[h], "x")

    DQ0 = {}
    r_dq, r_dks, r_dvs, r_dkx, r_dvx = {}, {}, {}, {}, {}
    attention_back(0)

    for e in (1, 3, 2):
        r_lh[e].wait_recv()
    lhz = LHB[0].astype(F32) + LHR[0].astype(F32) + LHR[1].astype(F32) + LHR[2].astype(F32)
    LHY[...] = lhz.astype(BF16)
    r_lhy = ring("y", lambda d: LHY, lambda e: LHYR.at[e - 1])
    cross(0)
    attention_back(1)

    for e in (1, 3, 2):
        r_lhy[e].wait_recv()
    lhy = lhz + LHYR[0].astype(F32) + LHYR[1].astype(F32) + LHYR[2].astype(F32)
    LHC[...] = lhy.astype(BF16)
    r_lhc = send(LHC, LHCR, "cfg")
    cross(1)
    attention_back(2)

    r_lhc.wait_recv()
    lhs = (lhy + LHCR[...].astype(F32)).astype(BF16)
    gup = nn(lhs, COT[0])
    for t in range(4):
        GSB[t, 0:16] = gup[t * 16:(t + 1) * 16].astype(BF16)
        for h in range(NH):
            GSB[t, 16:32, h * HD:(h + 1) * HD] = slope[h][t * 16:(t + 1) * 16].astype(BF16)
    r_gs = ring("z", lambda d: GSB.at[(z + d) % 4], lambda e: GSR.at[e - 1])
    cross(2)

    for e in (1, 3, 2):
        r_gs[e].wait_recv()
    s1 = GSB[z].astype(F32) + GSR[0].astype(F32) + GSR[1].astype(F32) + GSR[2].astype(F32)
    S1B[...] = s1.astype(BF16)
    r_s1 = [send(S1B, S1R.at[i], to) for i, to in enumerate(("sib", "x", "xo"))]
    for cp in r_s1:
        cp.wait_recv()
    s2 = s1 + S1R[0].astype(F32) + S1R[1].astype(F32) + S1R[2].astype(F32)
    S2B[...] = s2.astype(BF16)
    r_s2 = send(S2B, S2R, "cfg")
    r_s2.wait_recv()
    GU[0, 0, c] = S2B[0:16]
    GU[0, 0, 1 - c] = S2R[0:16]
    SL[0] = (s2[16:32] + S2R[16:32].astype(F32)).astype(BF16)
    r_gu = ring("y", lambda d: GU.at[0, 0], lambda e: GU.at[0, e])
    for e in (1, 3, 2):
        r_gu[e].wait_recv()
    r_guz = ring("z", lambda d: GU.at[0], lambda e: GU.at[e])
    r_sl = ring("z", lambda d: SL.at[0], lambda e: SL.at[e])

    for h in range(NH):
        hs = slice(h * HD, (h + 1) * HD)
        dq = DQ0[h]
        for e in (1, 3, 2):
            r_dq[h][e].wait_recv()
            dq += DQR[h, e - 1].astype(F32)
        dq_out[:, hs] = dq.T.astype(BF16)
        for out, own, near, far, r_near, r_far in (
            (dk_out, DK, DKR, DKXR, r_dks, r_dkx),
            (dv_out, DV, DVR, DVXR, r_dvs, r_dvx),
        ):
            r_near[h, 1].wait_recv()
            r_far[h].wait_recv()
            out[:, hs] = (own[h, 0:T] + near[h, 1].astype(F32) + far[h].astype(F32)).astype(BF16)

    for e in (1, 3, 2):
        r_guz[e].wait_recv()
        r_sl[e].wait_recv()
    for d in range(4):
        rows = pl.ds(pl.multiple_of(((z + d) % 4) * 16, 16), 16)
        SLT[rows] = SL[d].astype(F32)
        for j in range(4):
            for b in range(2):
                col = pl.multiple_of((((hy + j) % 4) * 2 + b) * W, 128)
                gup_out[rows, pl.ds(col, W)] = GU[d, j, b].astype(F32)
    slope_out[...] = SLT[...].T
    for cp in started:
        cp.wait_send()


def scratch():
    v = pltpu.VMEM
    return [
        v((4 * T, W), BF16),
        v((NK, W), BF16),
        v((NK, W), BF16),
        v((NH, HD, NK), BF16),
        v((NH, HD, NK), BF16),
        v((4, T, W), BF16),
        v((4, W + RANK, W), BF16),
        v((W, RANK), BF16),
        v((W + RANK, T), BF16),
        v((W + RANK, T), BF16),
        v((4, W + RANK, T), BF16),
        v((8, 8, T), F32),
        v((NH, NK, 4 * T), BF16),
        v((NH, 4, HD, T), F32),
        v((4, 8, T), F32),
        v((3, 4, 8, T), F32),
        v((NH, NK, HD), F32),
        v((NH, NK, HD), F32),
        v((NH, 4, HD, T), BF16),
        v((NH, 3, HD, T), BF16),
        v((NH, NK, HD), BF16),
        v((NH, NK, HD), BF16),
        v((NH, 2, T, HD), BF16),
        v((NH, 2, T, HD), BF16),
        v((NH, T, HD), BF16),
        v((NH, T, HD), BF16),
        v((NH, T, HD), BF16),
        v((NH, T, HD), BF16),
        v((4, RANK, T), BF16),
        v((3, RANK, T), BF16),
        v((RANK, T), BF16),
        v((3, RANK, T), BF16),
        v((RANK, T), BF16),
        v((RANK, T), BF16),
        v((4, 32, W), BF16),
        v((3, 32, W), BF16),
        v((32, W), BF16),
        v((3, 32, W), BF16),
        v((32, W), BF16),
        v((32, W), BF16),
        v((4, 4, 2, 16, W), BF16),
        v((4, 16, W), BF16),
        v((RANK, W), F32),
        pltpu.SemaphoreType.DMA((NSEM,)),
        pltpu.SemaphoreType.DMA((NSEM,)),
        pltpu.SemaphoreType.DMA((16,)),
    ]


def per_device(query, key, value, cotangent, slots, counts, guidance, weight, lowering, raising):
    hbm = pl.BlockSpec(memory_space=pl.ANY)
    smem = pl.BlockSpec(memory_space=pltpu.SMEM)
    vmem = pl.BlockSpec(memory_space=pltpu.VMEM)
    dq, dk, dv, slope, gup = pl.pallas_call(
        kernel,
        out_shape=(
            jax.ShapeDtypeStruct((T, W), BF16),
            jax.ShapeDtypeStruct((T, W), BF16),
            jax.ShapeDtypeStruct((T, W), BF16),
            jax.ShapeDtypeStruct((W, RANK), F32),
            jax.ShapeDtypeStruct((RANK, 8 * W), F32),
        ),
        in_specs=[hbm] * 7 + [smem] * 3,
        out_specs=(vmem,) * 5,
        scratch_shapes=scratch(),
        compiler_params=pltpu.CompilerParams(
            collective_id=0, has_side_effects=True, vmem_limit_bytes=56 * 2 ** 20
        ),
        cost_estimate=pl.CostEstimate(flops=10**10, bytes_accessed=8 * 10**6, transcendentals=3 * 10**6),
    )(query[0], key[0], value[0], cotangent, weight, lowering, raising, slots, counts, guidance)
    return dq[None], dk[None], dv[None], slope, gup


def solution(mesh):
    in_specs = (
        P("cfg", "seq", "head"),
        P("cfg", "seq", "head"),
        P("cfg", "seq", "head"),
        P("seq", ("head", "cfg")),
        P("seq", None),
        P("seq"),
        P(),
        P("head", None),
        P("head", None),
        P(),
    )
    out_specs = (
        P("cfg", "seq", "head"),
        P("cfg", "seq", "head"),
        P("cfg", "seq", "head"),
        P("head", None),
        P(),
    )
    return jax.shard_map(
        per_device, mesh=mesh, in_specs=in_specs, out_specs=out_specs, check_vma=False
    )
```

time: 502 us -> 89.4 us (0.18); the launches traced: 492 us -> 88.9 us
  blocking collectives: 145 us -> 0 us
  local copies, waits for them, and re-layouts: 138 us -> 10.2 us
  waiting for transfers between devices: 118 us -> 0 us
  Pallas kernels: 0 us -> 77.5 us
  other arithmetic: 43.6 us -> 0 us
  matrix products: 23.4 us -> 0 us
  between operations: 15.2 us -> 1.29 us
  loops' own time: 7.93 us -> 0 us
    psum x2 -> x0, blocking collectives: 145 us -> none  [the longest x1 127 us: per_device(): lax.psum(lowering_product.astype(jnp.bfloat16), ('seq', 'cfg'))]
    all_gather x3 -> x0, waiting for transfers between devices: 110 us -> none  [the longest x1 51.3 us: per_device(): grad_rows = lax.all_gather(cotangent, ('head', 'cfg'), axis=1, tiled=True)]
    pallas_call x0 -> x1, Pallas kernels: none -> 77.5 us  [per_device(): pl.pallas_call(kernel, out_shape=(jax.ShapeDtypeStruct((T, W), BF16), jax...]
    gather x12 -> x0, local copies, waits for them, and re-layouts: 50.5 us -> none  [the longest x8 27.5 us: scores(): k_tiles[ids]]
    scatter-add x4 -> x0, other arithmetic: 31.9 us -> none  [the longest x2 17.3 us: query_side(): dk_acc.at[ids]]
    dot_general x18 -> x0, matrix products: 22.2 us -> none  [the longest x2 4.06 us: query_side(): jnp.einsum('hqjk,qhd->jkhd', ds, q_tiles[i], preferred_element_type=thirt...]
    reshape x3 -> x0, local copies, waits for them, and re-layouts: 18 us -> none  [the longest x1 9.01 us: per_device(): v_tiles = values_all.reshape(-1, BLK, heads, HEAD_SIZE)]
    unnamed x22 -> x6, local copies, waits for them, and re-layouts: 27.6 us -> 10.2 us
  transfers between devices with their start and end apart: 6 -> 0, of which waited for: 4 -> 0; matrix products, arithmetic and copies ran while one was open for 31% -> 0% of each run, Pallas kernels for 0% -> 0%
where the time goes in v1:
time: 89.4 us; the launch traced here: 88.9 us
  Pallas kernels  77.5 us (87%)
  local copies, waits for them, and re-layouts  10.2 us (11%)
  between operations  1.29 us (1%)
    pallas_call x1, Pallas kernels, per_device(): pl.pallas_call(kernel, out_shape=(jax.ShapeDtypeStruct((T, W), BF16), jax...  77.5 us
    unnamed x6, local copies, waits for them, and re-layouts  10.2 us

profile of v1, /device:TPU:0, one launch (start us, length us, event | category | flops | bytes accessed | tf_op | source)
XLA Modules:
  0.0 88.9 jit_solution(16980224112287242428)
XLA Ops:
  1.3 1.5 %copy.15.low_in = bf16[384,64]{1,0:T(8,128)(2,1)} copy(bf16[384,64]{0,1:T(8,128)(2,1)} %param.18) | data formatting | bytes 98304 | tf_op args[8]
  2.8 77.5 %shard_map.137 = (bf16[256,384]{1,0:T(8,128)(2,1)}, bf16[256,384]{1,0:T(8,128)(2,1)}, bf16[256,384]{1,0:T(8,128)(2,1)}, f32[384,64]{1,0:T(8,128)}, f32[64,3072]{1,0:T(8,128)}) custom-call(bf16[256,384]{1,0:T(8,128)(2,1)} %bitcast.9, bf16[256,384]{1,0:T(8,128)(2,1)} %bitcast.10, bf16[256,384]{1,0:T(8,128)(2,1)} %bitcast.11, bf16[256,384]{1,0:T(8,128)(2,1)} %cot_in.1, ...), custom_call_target="tpu_custom_call" | custom-call | flops 10000000000 | bytes 8000000 | tf_op jit(solution)/shard_map/pallas_call | solution.py:379
  80.3 1.7 %copy.16 = f32[384,64]{0,1:T(8,128)} copy(f32[384,64]{1,0:T(8,128)} %get-tuple-element.18) | data formatting | bytes 196608
  82.0 1.6 %copy.22 = bf16[1,256,384]{2,1,0:T(8,128)(2,1)} copy(bf16[1,256,384]{2,1,0:T(8,128)(2,1)} %bitcast.8) | data formatting | bytes 393216
  83.6 1.6 %copy.23 = bf16[1,256,384]{2,1,0:T(8,128)(2,1)} copy(bf16[1,256,384]{2,1,0:T(8,128)(2,1)} %bitcast.7) | data formatting | bytes 393216
  85.2 1.6 %copy.24 = bf16[1,256,384]{2,1,0:T(8,128)(2,1)} copy(bf16[1,256,384]{2,1,0:T(8,128)(2,1)} %bitcast.6) | data formatting | bytes 393216
  86.8 2.1 %copy.25 = f32[64,3072]{1,0:T(8,128)} copy(f32[64,3072]{1,0:T(8,128)} %get-tuple-element.29) | data formatting | bytes 1572864

commit v2 on v1

v2 whole, which is shorter than its diff:
```python
import functools
import math

import jax
import jax.numpy as jnp
from jax import lax
from jax.experimental import pallas as pl
from jax.experimental.pallas import tpu as pltpu
from jax.sharding import PartitionSpec as P

HD = 128
NH = 3
W = 384
T = 256
NK = 1024
RANK = 64
SCALE = HD ** -0.5
C2 = SCALE * math.log2(math.e)
BIG = 3.0e38
F32 = jnp.float32
BF16 = jnp.bfloat16
MESH = pl.DeviceIdType.MESH
NSEM = 112


def nn(a, b):
    return lax.dot_general(a, b, (((1,), (0,)), ((), ())), preferred_element_type=F32)


def nt(a, b):
    return lax.dot_general(a, b, (((1,), (1,)), ((), ())), preferred_element_type=F32)


def tn(a, b):
    return lax.dot_general(a, b, (((0,), (0,)), ((), ())), preferred_element_type=F32)


def kernel(
    q_in, k_in, v_in, cot_in, w_in, low_in, up_in, slots_ref, counts_ref, guide_ref,
    dq_out, dk_out, dv_out, slope_out, gup_out,
    Q, K, V, KT, VT, COT, WB, LOW, PART, PARTR, DOT, BIAS, PR, OT, STO, STR, DLO, DLR,
    DK, DV, DQ, DQB, DQR, DKB, DVB, DKR, DVR, DKX, DVX, DKXR, DVXR,
    LHB, LHR, LHY, LHYR, GSB, GSR, S1, GU, SL,
    send_sem, recv_sem, loc_sem,
):
    s, hy, c = lax.axis_index("seq"), lax.axis_index("head"), lax.axis_index("cfg")
    z, x, kc = s // 4, (s // 2) % 2, s % 2
    g = s % 4
    plane = {
        "sib": z * 4 + x * 2 + (1 - kc),
        "x": z * 4 + (1 - x) * 2 + kc,
        "xo": z * 4 + (1 - x) * 2 + (1 - kc),
    }
    peer = {"cfg": {"cfg": 1 - c}}
    for d in (1, 2, 3):
        peer["z%d" % d] = {"seq": ((z + d) % 4) * 4 + g}
        peer["y%d" % d] = {"head": (hy + d) % 4}
        peer["cy%d" % d] = {"head": (hy + d) % 4, "cfg": 1 - c}
    for name, at in plane.items():
        peer[name] = {"seq": at}
        peer["c" + name] = {"seq": at, "cfg": 1 - c}

    count = [0, 0]
    started = []

    def local(src, dst):
        cp = pltpu.make_async_copy(src, dst, loc_sem.at[count[1]])
        count[1] += 1
        cp.start()
        return cp

    def send(src, dst, to):
        i = count[0]
        count[0] += 1
        cp = pltpu.make_async_remote_copy(
            src_ref=src, dst_ref=dst, send_sem=send_sem.at[i], recv_sem=recv_sem.at[i],
            device_id=peer[to], device_id_type=MESH,
        )
        cp.start()
        started.append(cp)
        return cp

    def ring(axis, src, dst):
        got = {}
        for d in (1, 3, 2):
            e = (4 - d) % 4
            got[e] = send(src(d), dst(e), "%s%d" % (axis, d))
        return got

    l_cot = local(cot_in, COT.at[0])
    l_w = []
    for j in range(4):
        col = pl.multiple_of((((hy + j) % 4) * 2 + c) * W, 128)
        l_w.append(local(w_in.at[:, pl.ds(col, W)], WB.at[j, pl.ds(RANK, W)]))
        l_w.append(local(up_in.at[:, pl.ds(col, W)], WB.at[j, pl.ds(0, RANK)]))
    l_kv = [local(k_in, K.at[pl.ds(0, T)]), local(v_in, V.at[pl.ds(0, T)])]
    l_q = local(q_in, Q.at[pl.ds(0, T)])
    l_low = local(low_in, LOW)

    barrier = pltpu.get_barrier_semaphore()
    for name in peer:
        pl.semaphore_signal(barrier, inc=1, device_id=peer[name], device_id_type=MESH)
    pl.semaphore_wait(barrier, len(peer))

    r_cot = ring("y", lambda d: cot_in, lambda e: COT.at[e])
    r_k = {}
    r_v = {}
    for to, r in (("sib", 1), ("x", 2)):
        r_k[r] = send(k_in, K.at[pl.ds(r * T, T)], to)
        r_v[r] = send(v_in, V.at[pl.ds(r * T, T)], to)
    r_q = ring("z", lambda d: q_in, lambda e: Q.at[pl.ds(e * T, T)])

    row = lax.broadcasted_iota(jnp.int32, (8, T), 0)
    lane = lax.broadcasted_iota(jnp.int32, (8, T), 1)
    rx, rk = row // 4, (row // 2) % 2
    gx = x + rx - 2 * x * rx
    gk = kc + rk - 2 * kc * rk
    base_block = 2 * (gx * 2 + gk) + row % 2
    for d in range(4):
        block = base_block + 8 * ((z + d) % 4)
        live = jnp.zeros((8, T), F32)
        for qb in range(2):
            n = counts_ref[qb]
            for j in range(16):
                want = jnp.where(j < n, slots_ref[qb, j], -1)
                hit = jnp.logical_and(block == want, lane // 128 == qb)
                live = jnp.where(hit, 1.0, live)
        BIAS[d] = jnp.where(live > 0, BIG, -BIG)
    r_bias = ring("z", lambda d: BIAS.at[d], lambda e: BIAS.at[4 + e])

    weight = 1.5 + 0.5 * guide_ref[0].astype(F32)
    coef = jnp.where(c == 0, weight, 1.0 - weight)

    first = {}

    def forward(d, half):
        ks = slice(half * NK // 2, (half + 1) * NK // 2)
        bias = BIAS[4 + d] if d else BIAS[0]
        bias = bias[half * 4:half * 4 + 4]
        for h in range(NH):
            hs = slice(h * HD, (h + 1) * HD)
            sc = nt(K[ks, hs], Q[d * T:(d + 1) * T, hs])
            sc = jnp.minimum(sc.reshape(4, 128, T), bias[:, None, :]).reshape(NK // 2, T)
            top = jnp.max(sc, axis=0, keepdims=True) * C2
            p = jnp.exp2(sc * C2 - top)
            total = jnp.sum(p, axis=0, keepdims=True)
            pb = p.astype(BF16)
            PR[h, ks, d * T:(d + 1) * T] = pb
            o = nn(VT[h, :, ks], pb)
            if half == 0:
                OT[h, d] = o
                first[h, d] = (top, total)
            else:
                top0, total0 = first[h, d]
                m = jnp.maximum(top, top0)
                a0, a1 = jnp.exp2(top0 - m), jnp.exp2(top - m)
                total = total0 * a0 + total * a1
                inv = 1.0 / total
                OT[h, d] = OT[h, d] * (a0 * inv) + o * (a1 * inv)
                STO[d, h:h + 1] = m + jnp.log2(total)
                tops[h, d] = (top0, top)
        if half == 1:
            STO[d, NH:] = jnp.zeros((8 - NH, T), F32)

    tops = {}
    for cp in l_kv:
        cp.wait()
    l_q.wait()
    r_k[1].wait_recv()
    r_v[1].wait_recv()
    for h in range(NH):
        VT[h, :, :NK // 2] = V[:NK // 2, h * HD:(h + 1) * HD].T
    forward(0, 0)
    for d in (1, 3):
        r_q[d].wait_recv()
        r_bias[d].wait_recv()
        forward(d, 0)

    l_cot.wait()
    for cp in l_w:
        cp.wait()
    for e in (1, 3, 2):
        r_cot[e].wait_recv()
    bands = [slice(0, RANK + HD), slice(RANK + HD, RANK + 2 * HD), slice(RANK + 2 * HD, RANK + 3 * HD)]
    r_part = []
    for band in bands:
        acc = nt(WB[0, band], COT[0]) + nt(WB[1, band], COT[1]) + nt(WB[2, band], COT[2]) + nt(WB[3, band], COT[3])
        PART[band] = acc.astype(BF16)
        r_part.append(send(PART.at[band], PARTR.at[band], "cfg"))

    r_k[2].wait_recv()
    r_k[3] = send(K.at[pl.ds(2 * T, T)], K.at[pl.ds(3 * T, T)], "sib")
    r_v[2].wait_recv()
    r_v[3] = send(V.at[pl.ds(2 * T, T)], V.at[pl.ds(3 * T, T)], "sib")
    l_low.wait()
    r_k[3].wait_recv()
    r_v[3].wait_recv()
    for h in range(NH):
        VT[h, :, NK // 2:] = V[NK // 2:, h * HD:(h + 1) * HD].T

    r_do = []
    for h, d in enumerate((0, 1, 3)):
        forward(d, 1)
        band = bands[h]
        r_part[h].wait_recv()
        base = (PART[band].astype(F32) + PARTR[band].astype(F32)) * coef
        if h == 0:
            dlh = base[:RANK].astype(BF16)
            DOT[0, :RANK] = dlh
            base = base[RANK:]
        hs = slice(h * HD, (h + 1) * HD)
        DOT[0, RANK + h * HD:RANK + (h + 1) * HD] = (base + tn(LOW[:, hs], dlh)).astype(BF16)
        r_do.append(ring("z", lambda d: DOT.at[0, band], lambda e: DOT.at[e, band]))
    r_q[2].wait_recv()
    r_bias[2].wait_recv()
    forward(2, 0)
    forward(2, 1)
    r_st = ring("z", lambda d: STO, lambda e: STR.at[e - 1])
    for h in range(NH):
        KT[h] = K[:, h * HD:(h + 1) * HD].T

    r_dl = []

    def send_delta(h):
        for d in range(4):
            if d:
                r_do[h][d].wait_recv()
            do = DOT[d, RANK + h * HD:RANK + (h + 1) * HD].astype(F32)
            DLO[h, d:d + 1] = jnp.sum(do * OT[h, d], axis=0, keepdims=True)
        DLO[h, 4:] = jnp.zeros((4, T), F32)
        r_dl.append(ring("z", lambda d: DLO.at[h], lambda e: DLR.at[h, e - 1]))

    send_delta(0)

    for e in (1, 3, 2):
        r_st[e].wait_recv()
    fac, share = {}, {}
    slope = [jnp.zeros((RANK, HD), F32) for _ in range(NH)]
    for d in (1, 3, 2, 0):
        lh = jnp.zeros((RANK, T), F32)
        for h in range(NH):
            parts = [STO[d, h:h + 1]] + [STR[e - 1, (d - e) % 4, h:h + 1] for e in (1, 2, 3)]
            top = functools.reduce(jnp.maximum, parts)
            ws = [jnp.exp2(p - top) for p in parts]
            inv = 1.0 / (ws[0] + ws[1] + ws[2] + ws[3])
            share[h, d] = [w * inv for w in ws]
            fac[h, d] = [jnp.exp2(m - top) * inv for m in tops[h, d]]
            ob = (OT[h, d] * share[h, d][0]).astype(BF16)
            lh += nn(LOW[:, h * HD:(h + 1) * HD], ob)
            slope[h] += nt(DOT[d, :RANK], ob)
        LHB[d] = (lh * coef).astype(BF16)
    r_lh = ring("z", lambda d: LHB.at[d], lambda e: LHR.at[e - 1])

    delta = {}

    def get_delta(h):
        for e in (1, 3, 2):
            r_dl[h][e].wait_recv()
        for d in range(4):
            dels = [DLO[h, d:d + 1]] + [DLR[h, e - 1, (d - e) % 4:(d - e) % 4 + 1] for e in (1, 2, 3)]
            delta[h, d] = functools.reduce(lambda a, b: a + b, [w * v for w, v in zip(share[h, d], dels)])

    r_dq, r_dks, r_dvs, r_dkx, r_dvx = {}, {}, {}, {}, {}

    def back(h, d):
        hs = slice(h * HD, (h + 1) * HD)
        qs = slice(d * T, (d + 1) * T)
        do = DOT[d, RANK + h * HD:RANK + (h + 1) * HD]
        dp = nn(V[:, hs], do)
        near = PR[h, :NK // 2, qs].astype(F32) * fac[h, d][0]
        far = PR[h, NK // 2:, qs].astype(F32) * fac[h, d][1]
        p = jnp.concatenate([near, far], axis=0)
        ds = (p * (dp - delta[h, d])).astype(BF16)
        dk = nn(ds, Q[d * T:(d + 1) * T, hs]) * SCALE
        dv = nt(p.astype(BF16), do)
        dq = nn(KT[h], ds) * SCALE
        if d == 0:
            DQ[h] = dq
        else:
            DQB[h, d] = dq.astype(BF16)
            r_dq[h, (4 - d) % 4] = send(DQB.at[h, d], DQR.at[h, 3 - d], "z%d" % d)
        return dk, dv

    def head_done(h, dk, dv):
        DK[h] = dk
        DV[h] = dv
        DKB[h] = dk.astype(BF16)
        DVB[h] = dv.astype(BF16)
        for r in (3, 1):
            rows = pl.ds(r * T, T)
            i = 0 if r == 3 else 1
            r_dks[h, r] = send(DKB.at[h, rows], DKR.at[h, i], "sib")
            r_dvs[h, r] = send(DVB.at[h, rows], DVR.at[h, i], "sib")

    def cross(h):
        rows = slice(2 * T, 3 * T)
        r_dks[h, 3].wait_recv()
        DKX[h] = (DK[h, rows] + DKR[h, 0].astype(F32)).astype(BF16)
        r_dkx[h] = send(DKX.at[h], DKXR.at[h], "x")
        r_dvs[h, 3].wait_recv()
        DVX[h] = (DV[h, rows] + DVR[h, 0].astype(F32)).astype(BF16)
        r_dvx[h] = send(DVX.at[h], DVXR.at[h], "x")

    def finish(h):
        hs = slice(h * HD, (h + 1) * HD)
        dq = DQ[h]
        for e in (1, 3, 2):
            r_dq[h, e].wait_recv()
            dq += DQR[h, e - 1].astype(F32)
        dq_out[:, hs] = dq.T.astype(BF16)
        for out, own, near, far, r_near, r_far in (
            (dk_out, DK, DKR, DKXR, r_dks, r_dkx),
            (dv_out, DV, DVR, DVXR, r_dvs, r_dvx),
        ):
            r_near[h, 1].wait_recv()
            r_far[h].wait_recv()
            out[:, hs] = (own[h, 0:T] + near[h, 1].astype(F32) + far[h].astype(F32)).astype(BF16)

    chain = {}

    def chain_lh():
        for e in (1, 3, 2):
            r_lh[e].wait_recv()
        lhz = LHB[0].astype(F32) + LHR[0].astype(F32) + LHR[1].astype(F32) + LHR[2].astype(F32)
        chain["lhz"] = lhz
        LHY[...] = lhz.astype(BF16)
        names = ("y1", "y3", "y2", "cfg", "cy1", "cy3", "cy2")
        chain["lhy"] = [send(LHY, LHYR.at[i], to) for i, to in enumerate(names)]

    def chain_gup():
        lhs = chain["lhz"]
        for i, cp in enumerate(chain["lhy"]):
            cp.wait_recv()
            lhs += LHYR[i].astype(F32)
        gup = nn(lhs.astype(BF16), COT[0])
        for t in range(4):
            GSB[t, 0:16] = gup[t * 16:(t + 1) * 16].astype(BF16)
            for h in range(NH):
                GSB[t, 16:32, h * HD:(h + 1) * HD] = slope[h][t * 16:(t + 1) * 16].astype(BF16)
        chain["gs"] = ring("z", lambda d: GSB.at[(z + d) % 4], lambda e: GSR.at[e - 1])

    def chain_plane():
        for e in (1, 3, 2):
            chain["gs"][e].wait_recv()
        s1 = GSB[z].astype(F32) + GSR[0].astype(F32) + GSR[1].astype(F32) + GSR[2].astype(F32)
        S1[c, g] = s1.astype(BF16)
        names = ("sib", "x", "xo", "cfg", "csib", "cx", "cxo")
        chain["s1"] = [send(S1.at[c, g], S1.at[c, g], to) for to in names]

    def chain_y():
        for cp in chain["s1"]:
            cp.wait_recv()
        both = []
        for b in range(2):
            both.append(S1[b, 0].astype(F32) + S1[b, 1].astype(F32) + S1[b, 2].astype(F32) + S1[b, 3].astype(F32))
            GU[0, 0, b] = both[b][0:16].astype(BF16)
        SL[0] = (both[0][16:32] + both[1][16:32]).astype(BF16)
        chain["gu"] = ring("y", lambda d: GU.at[0, 0], lambda e: GU.at[0, e])
        chain["sl"] = ring("z", lambda d: SL.at[0], lambda e: SL.at[e])

    def chain_z():
        for e in (1, 3, 2):
            chain["gu"][e].wait_recv()
        chain["guz"] = ring("z", lambda d: GU.at[0], lambda e: GU.at[e])

    def chain_end():
        for e in (1, 3, 2):
            chain["guz"][e].wait_recv()
            chain["sl"][e].wait_recv()
        for d in range(4):
            rows = pl.ds(pl.multiple_of(((z + d) % 4) * 16, 16), 16)
            slope_out[rows] = SL[d].astype(F32)
            for j in range(4):
                for b in range(2):
                    col = pl.multiple_of((((hy + j) % 4) * 2 + b) * W, 128)
                    gup_out[rows, pl.ds(col, W)] = GU[d, j, b].astype(F32)

    send_delta(1)
    get_delta(0)
    hooks = {
        (0, 1): [chain_lh],
        (0, 2): [lambda: send_delta(2)],
        (0, 3): [chain_gup, lambda: get_delta(1)],
        (1, 1): [lambda: cross(0), chain_plane],
        (1, 3): [lambda: get_delta(2)],
        (2, 0): [chain_y],
        (2, 1): [lambda: cross(1)],
        (2, 3): [chain_z],
    }
    for h in range(NH):
        dk, dv = None, None
        for step, d in enumerate((1, 3, 2, 0)):
            a, b = back(h, d)
            dk = a if dk is None else dk + a
            dv = b if dv is None else dv + b
            if step == 3:
                head_done(h, dk, dv)
            for hook in hooks.get((h, step), []):
                hook()
    finish(0)
    cross(2)
    finish(1)
    chain_end()
    finish(2)
    for cp in started:
        cp.wait_send()


def hand_over(*refs):
    n = len(refs) // 2
    for i in range(n):
        refs[n + i][...] = refs[i][...]


def scratch():
    v = pltpu.VMEM
    return [
        v((4 * T, W), BF16),
        v((NK, W), BF16),
        v((NK, W), BF16),
        v((NH, HD, NK), BF16),
        v((NH, HD, NK), BF16),
        v((4, T, W), BF16),
        v((4, W + RANK, W), BF16),
        v((RANK, W), BF16),
        v((W + RANK, T), BF16),
        v((W + RANK, T), BF16),
        v((4, W + RANK, T), BF16),
        v((8, 8, T), F32),
        v((NH, NK, 4 * T), BF16),
        v((NH, 4, HD, T), F32),
        v((4, 8, T), F32),
        v((3, 4, 8, T), F32),
        v((NH, 8, T), F32),
        v((NH, 3, 8, T), F32),
        v((NH, NK, HD), F32),
        v((NH, NK, HD), F32),
        v((NH, HD, T), F32),
        v((NH, 4, HD, T), BF16),
        v((NH, 3, HD, T), BF16),
        v((NH, NK, HD), BF16),
        v((NH, NK, HD), BF16),
        v((NH, 2, T, HD), BF16),
        v((NH, 2, T, HD), BF16),
        v((NH, T, HD), BF16),
        v((NH, T, HD), BF16),
        v((NH, T, HD), BF16),
        v((NH, T, HD), BF16),
        v((4, RANK, T), BF16),
        v((3, RANK, T), BF16),
        v((RANK, T), BF16),
        v((7, RANK, T), BF16),
        v((4, 32, W), BF16),
        v((3, 32, W), BF16),
        v((2, 4, 32, W), BF16),
        v((4, 4, 2, 16, W), BF16),
        v((4, 16, W), BF16),
        pltpu.SemaphoreType.DMA((NSEM,)),
        pltpu.SemaphoreType.DMA((NSEM,)),
        pltpu.SemaphoreType.DMA((16,)),
    ]


def per_device(query, key, value, cotangent, slots, counts, guidance, weight, lowering, raising):
    hbm = pl.BlockSpec(memory_space=pl.ANY)
    smem = pl.BlockSpec(memory_space=pltpu.SMEM)
    vmem = pl.BlockSpec(memory_space=pltpu.VMEM)
    shapes = (
        jax.ShapeDtypeStruct((T, W), BF16),
        jax.ShapeDtypeStruct((T, W), BF16),
        jax.ShapeDtypeStruct((T, W), BF16),
        jax.ShapeDtypeStruct((RANK, W), F32),
        jax.ShapeDtypeStruct((RANK, 8 * W), F32),
    )
    parts = pl.pallas_call(
        kernel,
        out_shape=shapes,
        in_specs=[hbm] * 7 + [smem] * 3,
        out_specs=(vmem,) * 5,
        scratch_shapes=scratch(),
        compiler_params=pltpu.CompilerParams(
            collective_id=0, has_side_effects=True, vmem_limit_bytes=56 * 2 ** 20
        ),
        cost_estimate=pl.CostEstimate(flops=10**10, bytes_accessed=8 * 10**6, transcendentals=3 * 10**6),
    )(query[0], key[0], value[0], cotangent, weight, lowering.T, raising, slots, counts, guidance)
    dq, dk, dv, slope, gup = pl.pallas_call(
        hand_over,
        out_shape=shapes,
        in_specs=[vmem] * 5,
        out_specs=(vmem,) * 5,
        cost_estimate=pl.CostEstimate(flops=0, bytes_accessed=4 * 10**6, transcendentals=0),
    )(*parts)
    return dq[None], dk[None], dv[None], slope.T, gup


def solution(mesh):
    in_specs = (
        P("cfg", "seq", "head"),
        P("cfg", "seq", "head"),
        P("cfg", "seq", "head"),
        P("seq", ("head", "cfg")),
        P("seq", None),
        P("seq"),
        P(),
        P("head", None),
        P("head", None),
        P(),
    )
    out_specs = (
        P("cfg", "seq", "head"),
        P("cfg", "seq", "head"),
        P("cfg", "seq", "head"),
        P("head", None),
        P(),
    )
    return jax.shard_map(
        per_device, mesh=mesh, in_specs=in_specs, out_specs=out_specs, check_vma=False
    )
```

time: 89.4 us -> 77.7 us (0.87)
  local copies, waits for them, and re-layouts: 10.2 us -> 0 us
  Pallas kernels: 77.5 us -> 76.2 us
    unnamed x6 -> x0, local copies, waits for them, and re-layouts: 10.2 us -> none
    pallas_call x1 -> x2, Pallas kernels: 77.5 us -> 76.2 us  [the longest x1 73.6 us: per_device(): pl.pallas_call(kernel, out_shape=shapes, in_specs=[hbm] * 7 + [smem] * 3,...]
where the time goes in v2:
time: 77.7 us; the launch traced here: 77.5 us
  Pallas kernels  76.2 us (98%)
  between operations  1.29 us (2%)
    pallas_call x1, Pallas kernels, per_device(): pl.pallas_call(kernel, out_shape=shapes, in_specs=[hbm] * 7 + [smem] * 3,...  73.6 us
    pallas_call x1, Pallas kernels, per_device(): pl.pallas_call(hand_over, out_shape=shapes, in_specs=[vmem] * 5, out_spec...  2.61 us

profile of v2, /device:TPU:0, one launch (start us, length us, event | category | flops | bytes accessed | tf_op | source)
XLA Modules:
  0.0 77.5 jit_solution(13388821312624096302)
XLA Ops:
  1.3 73.6 %shard_map.137 = (bf16[256,384]{1,0:T(8,128)(2,1)}, bf16[256,384]{1,0:T(8,128)(2,1)}, bf16[256,384]{1,0:T(8,128)(2,1)}, f32[64,384]{1,0:T(8,128)}, f32[64,3072]{1,0:T(8,128)}) custom-call(bf16[256,384]{1,0:T(8,128)(2,1)} %bitcast.8, bf16[256,384]{1,0:T(8,128)(2,1)} %bitcast.9, bf16[256,384]{1,0:T(8,128)(2,1)} %bitcast.10, bf16[256,384]{1,0:T(8,128)(2,1)} %cot_in.1, ...), custom_call_target="tpu_custom_call" | custom-call | flops 10000000000 | bytes 8000000 | tf_op jit(solution)/shard_map/pallas_call | solution.py:475
  74.9 2.6 %shard_map.138 = (bf16[256,384]{1,0:T(8,128)(2,1)}, bf16[256,384]{1,0:T(8,128)(2,1)}, bf16[256,384]{1,0:T(8,128)(2,1)}, f32[64,384]{1,0:T(8,128)}, f32[64,3072]{1,0:T(8,128)}) custom-call(bf16[256,384]{1,0:T(8,128)(2,1)} %get-tuple-element.15.refs_0_, bf16[256,384]{1,0:T(8,128)(2,1)} %get-tuple-element.16.refs_1_, ...), custom_call_target="tpu_custom_call" | custom-call | bytes 4000000 | tf_op jit(solution)/shard_map/pallas_call | solution.py:486

commit v3 on v2

--- a/solution.py
+++ b/solution.py
@@ -20,7 +20,7 @@
 F32 = jnp.float32
 BF16 = jnp.bfloat16
 MESH = pl.DeviceIdType.MESH
-NSEM = 112
+NSEM = 128
 
 
 def nn(a, b):
@@ -40,25 +40,29 @@
     dq_out, dk_out, dv_out, slope_out, gup_out,
     Q, K, V, KT, VT, COT, WB, LOW, PART, PARTR, DOT, BIAS, PR, OT, STO, STR, DLO, DLR,
     DK, DV, DQ, DQB, DQR, DKB, DVB, DKR, DVR, DKX, DVX, DKXR, DVXR,
-    LHB, LHR, LHY, LHYR, GSB, GSR, S1, GU, SL,
+    LHB, LHR, LHO, LHY, LHYR, GSB, GSR, S1, GU, SL,
     send_sem, recv_sem, loc_sem,
 ):
     s, hy, c = lax.axis_index("seq"), lax.axis_index("head"), lax.axis_index("cfg")
     z, x, kc = s // 4, (s // 2) % 2, s % 2
     g = s % 4
-    plane = {
-        "sib": z * 4 + x * 2 + (1 - kc),
-        "x": z * 4 + (1 - x) * 2 + kc,
-        "xo": z * 4 + (1 - x) * 2 + (1 - kc),
-    }
+    px = [x, x, 1 - x, 1 - x]
+    pk = [kc, 1 - kc, kc, 1 - kc]
     peer = {"cfg": {"cfg": 1 - c}}
+    for r in range(4):
+        for d in range(4):
+            if r or d:
+                peer["s%d%d" % (d, r)] = {"seq": ((z + d) % 4) * 4 + px[r] * 2 + pk[r]}
+        if r:
+            peer["c%d" % r] = {"seq": z * 4 + px[r] * 2 + pk[r], "cfg": 1 - c}
     for d in (1, 2, 3):
-        peer["z%d" % d] = {"seq": ((z + d) % 4) * 4 + g}
         peer["y%d" % d] = {"head": (hy + d) % 4}
         peer["cy%d" % d] = {"head": (hy + d) % 4, "cfg": 1 - c}
-    for name, at in plane.items():
-        peer[name] = {"seq": at}
-        peer["c" + name] = {"seq": at, "cfg": 1 - c}
+        for t in (1, 2, 3):
+            peer["yz%d%d" % (d, t)] = {"head": (hy + d) % 4, "seq": ((z + t) % 4) * 4 + g}
+    for name, alias in (("sib", "s01"), ("x", "s02"), ("xo", "s03"), ("z1", "s10"), ("z2", "s20"), ("z3", "s30")):
+        peer[name] = peer[alias]
+    everyone = [name for name in peer if name not in ("sib", "x", "xo", "z1", "z2", "z3")]
 
     count = [0, 0]
     started = []
@@ -98,9 +102,9 @@
     l_low = local(low_in, LOW)
 
     barrier = pltpu.get_barrier_semaphore()
-    for name in peer:
+    for name in everyone:
         pl.semaphore_signal(barrier, inc=1, device_id=peer[name], device_id_type=MESH)
-    pl.semaphore_wait(barrier, len(peer))
+    pl.semaphore_wait(barrier, len(everyone))
 
     r_cot = ring("y", lambda d: cot_in, lambda e: COT.at[e])
     r_k = {}
@@ -108,7 +112,7 @@
     for to, r in (("sib", 1), ("x", 2)):
         r_k[r] = send(k_in, K.at[pl.ds(r * T, T)], to)
         r_v[r] = send(v_in, V.at[pl.ds(r * T, T)], to)
-    r_q = ring("z", lambda d: q_in, lambda e: Q.at[pl.ds(e * T, T)])
+    r_q = {4 - d: send(q_in, Q.at[pl.ds((4 - d) * T, T)], "z%d" % d) for d in (1, 3)}
 
     row = lax.broadcasted_iota(jnp.int32, (8, T), 0)
     lane = lax.broadcasted_iota(jnp.int32, (8, T), 1)
@@ -157,12 +161,17 @@
                 total = total0 * a0 + total * a1
                 inv = 1.0 / total
                 OT[h, d] = OT[h, d] * (a0 * inv) + o * (a1 * inv)
-                STO[d, h:h + 1] = m + jnp.log2(total)
+                STO[4 * h + d:4 * h + d + 1] = m + jnp.log2(total)
                 tops[h, d] = (top0, top)
-        if half == 1:
-            STO[d, NH:] = jnp.zeros((8 - NH, T), F32)
-
-    tops = {}
+                low = nn(LOW[:, hs], OT[h, d].astype(BF16))
+                if d:
+                    LHB[d, h * RANK:(h + 1) * RANK] = low.astype(BF16)
+                else:
+                    LHO[h] = low
+        if half and d:
+            r_lh[(4 - d) % 4] = send(LHB.at[d], LHR.at[3 - d], "z%d" % d)
+
+    tops, r_lh = {}, {}
     for cp in l_kv:
         cp.wait()
     l_q.wait()
@@ -173,14 +182,27 @@
     forward(0, 0)
     for d in (1, 3):
         r_q[d].wait_recv()
+    far_q = [
+        send(Q.at[pl.ds(3 * T, T // 2)], Q.at[pl.ds(2 * T, T // 2)], "z1"),
+        send(Q.at[pl.ds(T + T // 2, T // 2)], Q.at[pl.ds(2 * T + T // 2, T // 2)], "z3"),
+    ]
+    for d in (1, 3):
         r_bias[d].wait_recv()
         forward(d, 0)
+    for cp in far_q:
+        cp.wait_recv()
+    r_bias[2].wait_recv()
+    forward(2, 0)
 
     l_cot.wait()
     for cp in l_w:
         cp.wait()
     for e in (1, 3, 2):
         r_cot[e].wait_recv()
+    r_k[2].wait_recv()
+    r_k[3] = send(K.at[pl.ds(2 * T, T)], K.at[pl.ds(3 * T, T)], "sib")
+    r_v[2].wait_recv()
+    r_v[3] = send(V.at[pl.ds(2 * T, T)], V.at[pl.ds(3 * T, T)], "sib")
     bands = [slice(0, RANK + HD), slice(RANK + HD, RANK + 2 * HD), slice(RANK + 2 * HD, RANK + 3 * HD)]
     r_part = []
     for band in bands:
@@ -188,68 +210,91 @@
         PART[band] = acc.astype(BF16)
         r_part.append(send(PART.at[band], PARTR.at[band], "cfg"))
 
-    r_k[2].wait_recv()
-    r_k[3] = send(K.at[pl.ds(2 * T, T)], K.at[pl.ds(3 * T, T)], "sib")
-    r_v[2].wait_recv()
-    r_v[3] = send(V.at[pl.ds(2 * T, T)], V.at[pl.ds(3 * T, T)], "sib")
-    l_low.wait()
     r_k[3].wait_recv()
     r_v[3].wait_recv()
     for h in range(NH):
         VT[h, :, NK // 2:] = V[NK // 2:, h * HD:(h + 1) * HD].T
 
+    l_low.wait()
     r_do = []
-    for h, d in enumerate((0, 1, 3)):
-        forward(d, 1)
+
+    def send_do(h):
         band = bands[h]
         r_part[h].wait_recv()
         base = (PART[band].astype(F32) + PARTR[band].astype(F32)) * coef
         if h == 0:
-            dlh = base[:RANK].astype(BF16)
-            DOT[0, :RANK] = dlh
+            DOT[0, :RANK] = base[:RANK].astype(BF16)
             base = base[RANK:]
         hs = slice(h * HD, (h + 1) * HD)
-        DOT[0, RANK + h * HD:RANK + (h + 1) * HD] = (base + tn(LOW[:, hs], dlh)).astype(BF16)
-        r_do.append(ring("z", lambda d: DOT.at[0, band], lambda e: DOT.at[e, band]))
-    r_q[2].wait_recv()
-    r_bias[2].wait_recv()
-    forward(2, 0)
+        DOT[0, RANK + h * HD:RANK + (h + 1) * HD] = (base + tn(LOW[:, hs], DOT[0, :RANK])).astype(BF16)
+        r_do.append({4 - d: send(DOT.at[0, band], DOT.at[4 - d, band], "z%d" % d) for d in (1, 3)})
+
     forward(2, 1)
+    forward(1, 1)
+    send_do(0)
+    forward(3, 1)
+    send_do(1)
+    forward(0, 1)
+    STO[4 * NH:] = jnp.zeros((16 - 4 * NH, T), F32)
     r_st = ring("z", lambda d: STO, lambda e: STR.at[e - 1])
+    send_do(2)
     for h in range(NH):
         KT[h] = K[:, h * HD:(h + 1) * HD].T
 
     r_dl = []
 
+    def relay_do(h):
+        lo, n = bands[h].start, bands[h].stop - bands[h].start
+        one = pl.ds(lo, n // 2)
+        two = pl.ds(lo + n // 2, n // 2)
+        r_do[h][3].wait_recv()
+        a = send(DOT.at[3, one], DOT.at[2, one], "z1")
+        r_do[h][1].wait_recv()
+        b = send(DOT.at[1, two], DOT.at[2, two], "z3")
+        r_do[h][2] = [a, b]
+
     def send_delta(h):
-        for d in range(4):
-            if d:
-                r_do[h][d].wait_recv()
+        for d in (0, 1, 3, 2):
+            if d == 2:
+                for cp in r_do[h][2]:
+                    cp.wait_recv()
             do = DOT[d, RANK + h * HD:RANK + (h + 1) * HD].astype(F32)
             DLO[h, d:d + 1] = jnp.sum(do * OT[h, d], axis=0, keepdims=True)
         DLO[h, 4:] = jnp.zeros((4, T), F32)
         r_dl.append(ring("z", lambda d: DLO.at[h], lambda e: DLR.at[h, e - 1]))
 
-    send_delta(0)
-
+    relay_do(0)
     for e in (1, 3, 2):
         r_st[e].wait_recv()
     fac, share = {}, {}
-    slope = [jnp.zeros((RANK, HD), F32) for _ in range(NH)]
-    for d in (1, 3, 2, 0):
-        lh = jnp.zeros((RANK, T), F32)
+    for d in (0, 1, 3, 2):
         for h in range(NH):
-            parts = [STO[d, h:h + 1]] + [STR[e - 1, (d - e) % 4, h:h + 1] for e in (1, 2, 3)]
+            parts = [STO[4 * h + d:4 * h + d + 1]]
+            for e in (1, 2, 3):
+                i = 4 * h + (d - e) % 4
+                parts.append(STR[e - 1, i:i + 1])
             top = functools.reduce(jnp.maximum, parts)
             ws = [jnp.exp2(p - top) for p in parts]
             inv = 1.0 / (ws[0] + ws[1] + ws[2] + ws[3])
             share[h, d] = [w * inv for w in ws]
             fac[h, d] = [jnp.exp2(m - top) * inv for m in tops[h, d]]
-            ob = (OT[h, d] * share[h, d][0]).astype(BF16)
-            lh += nn(LOW[:, h * HD:(h + 1) * HD], ob)
-            slope[h] += nt(DOT[d, :RANK], ob)
-        LHB[d] = (lh * coef).astype(BF16)
-    r_lh = ring("z", lambda d: LHB.at[d], lambda e: LHR.at[e - 1])
+        if d == 0:
+            lhz = functools.reduce(lambda a, b: a + b, [LHO[h] * share[h, 0][0] for h in range(NH)])
+            for e in (1, 3, 2):
+                r_lh[e].wait_recv()
+                for h in range(NH):
+                    lhz += LHR[e - 1, h * RANK:(h + 1) * RANK].astype(F32) * share[h, 0][e]
+            lhz = lhz * coef
+            LHY[...] = lhz.astype(BF16)
+            names = ("y1", "y3", "y2", "cfg", "cy1", "cy3", "cy2")
+            r_lhy = [send(LHY, LHYR.at[i], to) for i, to in enumerate(names)]
+    relay_do(1)
+    send_delta(0)
+    relay_do(2)
+    slope = [jnp.zeros((RANK, HD), F32) for _ in range(NH)]
+    for d in (0, 1, 3, 2):
+        for h in range(NH):
+            slope[h] += nt(DOT[d, :RANK], (OT[h, d] * share[h, d][0]).astype(BF16))
 
     delta = {}
 
@@ -262,35 +307,37 @@
 
     r_dq, r_dks, r_dvs, r_dkx, r_dvx = {}, {}, {}, {}, {}
 
-    def back(h, d):
+    def back(h, half, d):
         hs = slice(h * HD, (h + 1) * HD)
+        ks = slice(half * NK // 2, (half + 1) * NK // 2)
         qs = slice(d * T, (d + 1) * T)
         do = DOT[d, RANK + h * HD:RANK + (h + 1) * HD]
-        dp = nn(V[:, hs], do)
-        near = PR[h, :NK // 2, qs].astype(F32) * fac[h, d][0]
-        far = PR[h, NK // 2:, qs].astype(F32) * fac[h, d][1]
-        p = jnp.concatenate([near, far], axis=0)
+        dp = nn(V[ks, hs], do)
+        p = PR[h, ks, qs].astype(F32) * fac[h, d][half]
         ds = (p * (dp - delta[h, d])).astype(BF16)
-        dk = nn(ds, Q[d * T:(d + 1) * T, hs]) * SCALE
+        dk = nn(ds, Q[qs, hs]) * SCALE
         dv = nt(p.astype(BF16), do)
-        dq = nn(KT[h], ds) * SCALE
-        if d == 0:
-            DQ[h] = dq
+        dq = nn(KT[h, :, ks], ds) * SCALE
+        if half == 1:
+            DQ[h, d] = dq
         else:
-            DQB[h, d] = dq.astype(BF16)
-            r_dq[h, (4 - d) % 4] = send(DQB.at[h, d], DQR.at[h, 3 - d], "z%d" % d)
+            dq += DQ[h, d]
+            if d == 0:
+                DQ[h, 0] = dq
+            else:
+                DQB[h, d] = dq.astype(BF16)
+                r_dq[h, (4 - d) % 4] = send(DQB.at[h, d], DQR.at[h, 3 - d], "z%d" % d)
         return dk, dv
 
-    def head_done(h, dk, dv):
-        DK[h] = dk
-        DV[h] = dv
-        DKB[h] = dk.astype(BF16)
-        DVB[h] = dv.astype(BF16)
-        for r in (3, 1):
-            rows = pl.ds(r * T, T)
-            i = 0 if r == 3 else 1
-            r_dks[h, r] = send(DKB.at[h, rows], DKR.at[h, i], "sib")
-            r_dvs[h, r] = send(DVB.at[h, rows], DVR.at[h, i], "sib")
+    def half_done(h, half, dk, dv):
+        ks = slice(half * NK // 2, (half + 1) * NK // 2)
+        DK[h, ks] = dk
+        DV[h, ks] = dv
+        r = 1 + 2 * half
+        DKB[h, half] = dk[T:].astype(BF16)
+        DVB[h, half] = dv[T:].astype(BF16)
+        r_dks[h, r] = send(DKB.at[h, half], DKR.at[h, 1 - half], "sib")
+        r_dvs[h, r] = send(DVB.at[h, half], DVR.at[h, 1 - half], "sib")
 
     def cross(h):
         rows = slice(2 * T, 3 * T)
@@ -303,7 +350,7 @@
 
     def finish(h):
         hs = slice(h * HD, (h + 1) * HD)
-        dq = DQ[h]
+        dq = DQ[h, 0]
         for e in (1, 3, 2):
             r_dq[h, e].wait_recv()
             dq += DQR[h, e - 1].astype(F32)
@@ -318,52 +365,51 @@
 
     chain = {}
 
-    def chain_lh():
-        for e in (1, 3, 2):
-            r_lh[e].wait_recv()
-        lhz = LHB[0].astype(F32) + LHR[0].astype(F32) + LHR[1].astype(F32) + LHR[2].astype(F32)
-        chain["lhz"] = lhz
-        LHY[...] = lhz.astype(BF16)
-        names = ("y1", "y3", "y2", "cfg", "cy1", "cy3", "cy2")
-        chain["lhy"] = [send(LHY, LHYR.at[i], to) for i, to in enumerate(names)]
-
     def chain_gup():
-        lhs = chain["lhz"]
-        for i, cp in enumerate(chain["lhy"]):
+        lhs = lhz
+        for i, cp in enumerate(r_lhy):
             cp.wait_recv()
             lhs += LHYR[i].astype(F32)
         gup = nn(lhs.astype(BF16), COT[0])
-        for t in range(4):
-            GSB[t, 0:16] = gup[t * 16:(t + 1) * 16].astype(BF16)
+        for t in range(16):
+            GSB[t, 0:4] = gup[t * 4:(t + 1) * 4]
             for h in range(NH):
-                GSB[t, 16:32, h * HD:(h + 1) * HD] = slope[h][t * 16:(t + 1) * 16].astype(BF16)
-        chain["gs"] = ring("z", lambda d: GSB.at[(z + d) % 4], lambda e: GSR.at[e - 1])
+                GSB[t, 4:8, h * HD:(h + 1) * HD] = slope[h][t * 4:(t + 1) * 4]
+        chain["gs"] = []
+        for d in (1, 3, 2, 0):
+            for r in range(4):
+                if r or d:
+                    i = ((4 - d) % 4) * 4 + r
+                    to = ((z + d) % 4) * 4 + px[r] * 2 + pk[r]
+                    chain["gs"].append(send(GSB.at[to], GSR.at[i], "s%d%d" % (d, r)))
 
     def chain_plane():
-        for e in (1, 3, 2):
-            chain["gs"][e].wait_recv()
-        s1 = GSB[z].astype(F32) + GSR[0].astype(F32) + GSR[1].astype(F32) + GSR[2].astype(F32)
-        S1[c, g] = s1.astype(BF16)
-        names = ("sib", "x", "xo", "cfg", "csib", "cx", "cxo")
+        for cp in chain["gs"]:
+            cp.wait_recv()
+        s1 = GSB[s]
+        for i in range(1, 16):
+            s1 += GSR[i]
+        S1[c, g] = s1
+        names = ("sib", "x", "xo", "cfg", "c1", "c2", "c3")
         chain["s1"] = [send(S1.at[c, g], S1.at[c, g], to) for to in names]
 
-    def chain_y():
+    def chain_yz():
         for cp in chain["s1"]:
             cp.wait_recv()
-        both = []
         for b in range(2):
-            both.append(S1[b, 0].astype(F32) + S1[b, 1].astype(F32) + S1[b, 2].astype(F32) + S1[b, 3].astype(F32))
-            GU[0, 0, b] = both[b][0:16].astype(BF16)
-        SL[0] = (both[0][16:32] + both[1][16:32]).astype(BF16)
+            GU[0, 0, b] = jnp.concatenate([S1[b, i, 0:4] for i in range(4)], axis=0).astype(BF16)
+        SL[0] = jnp.concatenate([S1[0, i, 4:8] + S1[1, i, 4:8] for i in range(4)], axis=0).astype(BF16)
+        chain["sl"] = ring("z", lambda d: SL.at[0], lambda e: SL.at[e])
         chain["gu"] = ring("y", lambda d: GU.at[0, 0], lambda e: GU.at[0, e])
-        chain["sl"] = ring("z", lambda d: SL.at[0], lambda e: SL.at[e])
-
-    def chain_z():
-        for e in (1, 3, 2):
-            chain["gu"][e].wait_recv()
-        chain["guz"] = ring("z", lambda d: GU.at[0], lambda e: GU.at[e])
+        chain["guz"] = ring("z", lambda d: GU.at[0, 0], lambda e: GU.at[e, 0])
+        for d in (1, 3, 2):
+            for t in (1, 3, 2):
+                cp = send(GU.at[0, 0], GU.at[4 - t, 4 - d], "yz%d%d" % (d, t))
+                chain["gu"][4 * d + t] = cp
 
     def chain_end():
+        for cp in chain["gu"].values():
+            cp.wait_recv()
         for e in (1, 3, 2):
             chain["guz"][e].wait_recv()
             chain["sl"][e].wait_recv()
@@ -375,33 +421,33 @@
                     col = pl.multiple_of((((hy + j) % 4) * 2 + b) * W, 128)
                     gup_out[rows, pl.ds(col, W)] = GU[d, j, b].astype(F32)
 
-    send_delta(1)
     get_delta(0)
     hooks = {
-        (0, 1): [chain_lh],
-        (0, 2): [lambda: send_delta(2)],
-        (0, 3): [chain_gup, lambda: get_delta(1)],
-        (1, 1): [lambda: cross(0), chain_plane],
-        (1, 3): [lambda: get_delta(2)],
-        (2, 0): [chain_y],
-        (2, 1): [lambda: cross(1)],
-        (2, 3): [chain_z],
+        (0, 1, 1): [lambda: send_delta(1), chain_gup],
+        (0, 1, 3): [lambda: send_delta(2)],
+        (0, 0, 1): [lambda: cross(0)],
+        (0, 0, 3): [lambda: get_delta(1)],
+        (1, 1, 3): [chain_plane],
+        (1, 0, 1): [lambda: cross(1)],
+        (1, 0, 3): [lambda: get_delta(2)],
+        (2, 1, 3): [chain_yz],
+        (2, 0, 1): [lambda: cross(2)],
     }
     for h in range(NH):
-        dk, dv = None, None
-        for step, d in enumerate((1, 3, 2, 0)):
-            a, b = back(h, d)
-            dk = a if dk is None else dk + a
-            dv = b if dv is None else dv + b
-            if step == 3:
-                head_done(h, dk, dv)
-            for hook in hooks.get((h, step), []):
-                hook()
+        for half in (1, 0):
+            dk, dv = None, None
+            for step, d in enumerate((1, 3, 2, 0)):
+                a, b = back(h, half, d)
+                dk = a if dk is None else dk + a
+                dv = b if dv is None else dv + b
+                if step == 3:
+                    half_done(h, half, dk, dv)
+                for hook in hooks.get((h, half, step), []):
+                    hook()
     finish(0)
-    cross(2)
     finish(1)
+    finish(2)
     chain_end()
-    finish(2)
     for cp in started:
         cp.wait_send()
 
@@ -429,30 +475,31 @@
         v((8, 8, T), F32),
         v((NH, NK, 4 * T), BF16),
         v((NH, 4, HD, T), F32),
-        v((4, 8, T), F32),
-        v((3, 4, 8, T), F32),
+        v((16, T), F32),
+        v((3, 16, T), F32),
         v((NH, 8, T), F32),
         v((NH, 3, 8, T), F32),
         v((NH, NK, HD), F32),
         v((NH, NK, HD), F32),
-        v((NH, HD, T), F32),
+        v((NH, 4, HD, T), F32),
         v((NH, 4, HD, T), BF16),
         v((NH, 3, HD, T), BF16),
-        v((NH, NK, HD), BF16),
-        v((NH, NK, HD), BF16),
+        v((NH, 2, T, HD), BF16),
+        v((NH, 2, T, HD), BF16),
         v((NH, 2, T, HD), BF16),
         v((NH, 2, T, HD), BF16),
         v((NH, T, HD), BF16),
         v((NH, T, HD), BF16),
         v((NH, T, HD), BF16),
         v((NH, T, HD), BF16),
-        v((4, RANK, T), BF16),
-        v((3, RANK, T), BF16),
+        v((4, NH * RANK, T), BF16),
+        v((3, NH * RANK, T), BF16),
+        v((NH, RANK, T), F32),
         v((RANK, T), BF16),
         v((7, RANK, T), BF16),
-        v((4, 32, W), BF16),
-        v((3, 32, W), BF16),
-        v((2, 4, 32, W), BF16),
+        v((16, 8, W), F32),
+        v((16, 8, W), F32),
+        v((2, 4, 8, W), F32),
         v((4, 4, 2, 16, W), BF16),
         v((4, 16, W), BF16),
         pltpu.SemaphoreType.DMA((NSEM,)),

time: 77.7 us -> 71.3 us (0.918)
  Pallas kernels: 76.2 us -> 69.4 us
    pallas_call x1, Pallas kernels: 73.6 us -> 66.8 us  [per_device(): pl.pallas_call(kernel, out_shape=shapes, in_specs=[hbm] * 7 + [smem] * 3,...]
where the time goes in v3:
time: 71.3 us; the launch traced here: 70.7 us
  Pallas kernels  69.4 us (97%)
  between operations  1.29 us (2%)
    pallas_call x1, Pallas kernels, per_device(): pl.pallas_call(kernel, out_shape=shapes, in_specs=[hbm] * 7 + [smem] * 3,...  66.8 us
    pallas_call x1, Pallas kernels, per_device(): pl.pallas_call(hand_over, out_shape=shapes, in_specs=[vmem] * 5, out_spec...  2.61 us

profile of v3, /device:TPU:0, one launch (start us, length us, event | category | flops | bytes accessed | tf_op | source)
XLA Modules:
  0.0 70.7 jit_solution(1606895677963661803)
XLA Ops:
  1.3 66.8 %shard_map.137 = (bf16[256,384]{1,0:T(8,128)(2,1)}, bf16[256,384]{1,0:T(8,128)(2,1)}, bf16[256,384]{1,0:T(8,128)(2,1)}, f32[64,384]{1,0:T(8,128)}, f32[64,3072]{1,0:T(8,128)}) custom-call(bf16[256,384]{1,0:T(8,128)(2,1)} %bitcast.8, bf16[256,384]{1,0:T(8,128)(2,1)} %bitcast.9, bf16[256,384]{1,0:T(8,128)(2,1)} %bitcast.10, bf16[256,384]{1,0:T(8,128)(2,1)} %cot_in.1, ...), custom_call_target="tpu_custom_call" | custom-call | flops 10000000000 | bytes 8000000 | tf_op jit(solution)/shard_map/pallas_call | solution.py:522
  68.1 2.6 %shard_map.138 = (bf16[256,384]{1,0:T(8,128)(2,1)}, bf16[256,384]{1,0:T(8,128)(2,1)}, bf16[256,384]{1,0:T(8,128)(2,1)}, f32[64,384]{1,0:T(8,128)}, f32[64,3072]{1,0:T(8,128)}) custom-call(bf16[256,384]{1,0:T(8,128)(2,1)} %get-tuple-element.15.refs_0_, bf16[256,384]{1,0:T(8,128)(2,1)} %get-tuple-element.16.refs_1_, ...), custom_call_target="tpu_custom_call" | custom-call | bytes 4000000 | tf_op jit(solution)/shard_map/pallas_call | solution.py:533

commit v4 on v3

--- a/solution.py
+++ b/solution.py
@@ -51,13 +51,12 @@
     peer = {"cfg": {"cfg": 1 - c}}
     for r in range(4):
         for d in range(4):
-            if r or d:
+            if (r == 0) != (d == 0):
                 peer["s%d%d" % (d, r)] = {"seq": ((z + d) % 4) * 4 + px[r] * 2 + pk[r]}
         if r:
             peer["c%d" % r] = {"seq": z * 4 + px[r] * 2 + pk[r], "cfg": 1 - c}
     for d in (1, 2, 3):
         peer["y%d" % d] = {"head": (hy + d) % 4}
-        peer["cy%d" % d] = {"head": (hy + d) % 4, "cfg": 1 - c}
         for t in (1, 2, 3):
             peer["yz%d%d" % (d, t)] = {"head": (hy + d) % 4, "seq": ((z + t) % 4) * 4 + g}
     for name, alias in (("sib", "s01"), ("x", "s02"), ("xo", "s03"), ("z1", "s10"), ("z2", "s20"), ("z3", "s30")):
@@ -106,7 +105,7 @@
         pl.semaphore_signal(barrier, inc=1, device_id=peer[name], device_id_type=MESH)
     pl.semaphore_wait(barrier, len(everyone))
 
-    r_cot = ring("y", lambda d: cot_in, lambda e: COT.at[e])
+    r_cot = {4 - d: send(cot_in, COT.at[4 - d], "y%d" % d) for d in (1, 3)}
     r_k = {}
     r_v = {}
     for to, r in (("sib", 1), ("x", 2)):
@@ -181,35 +180,42 @@
         VT[h, :, :NK // 2] = V[:NK // 2, h * HD:(h + 1) * HD].T
     forward(0, 0)
     for d in (1, 3):
+        r_cot[d].wait_recv()
+    head, tail = pl.ds(0, T // 2), pl.ds(T // 2, T // 2)
+    far_cot = [
+        send(COT.at[3, head], COT.at[2, head], "y1"),
+        send(COT.at[1, tail], COT.at[2, tail], "y3"),
+    ]
+    for d in (1, 3):
         r_q[d].wait_recv()
     far_q = [
         send(Q.at[pl.ds(3 * T, T // 2)], Q.at[pl.ds(2 * T, T // 2)], "z1"),
         send(Q.at[pl.ds(T + T // 2, T // 2)], Q.at[pl.ds(2 * T + T // 2, T // 2)], "z3"),
     ]
+    l_cot.wait()
+    for cp in l_w:
+        cp.wait()
+    bands = [slice(0, RANK + HD), slice(RANK + HD, RANK + 2 * HD), slice(RANK + 2 * HD, RANK + 3 * HD)]
+    accs = [nt(WB[0, b], COT[0]) + nt(WB[1, b], COT[1]) + nt(WB[3, b], COT[3]) for b in bands]
     for d in (1, 3):
         r_bias[d].wait_recv()
         forward(d, 0)
+
+    r_k[2].wait_recv()
+    r_k[3] = send(K.at[pl.ds(2 * T, T)], K.at[pl.ds(3 * T, T)], "sib")
+    r_v[2].wait_recv()
+    r_v[3] = send(V.at[pl.ds(2 * T, T)], V.at[pl.ds(3 * T, T)], "sib")
+    for cp in far_cot:
+        cp.wait_recv()
+    r_part = []
+    for band, acc in zip(bands, accs):
+        PART[band] = (acc + nt(WB[2, band], COT[2])).astype(BF16)
+        r_part.append(send(PART.at[band], PARTR.at[band], "cfg"))
+
     for cp in far_q:
         cp.wait_recv()
     r_bias[2].wait_recv()
     forward(2, 0)
-
-    l_cot.wait()
-    for cp in l_w:
-        cp.wait()
-    for e in (1, 3, 2):
-        r_cot[e].wait_recv()
-    r_k[2].wait_recv()
-    r_k[3] = send(K.at[pl.ds(2 * T, T)], K.at[pl.ds(3 * T, T)], "sib")
-    r_v[2].wait_recv()
-    r_v[3] = send(V.at[pl.ds(2 * T, T)], V.at[pl.ds(3 * T, T)], "sib")
-    bands = [slice(0, RANK + HD), slice(RANK + HD, RANK + 2 * HD), slice(RANK + 2 * HD, RANK + 3 * HD)]
-    r_part = []
-    for band in bands:
-        acc = nt(WB[0, band], COT[0]) + nt(WB[1, band], COT[1]) + nt(WB[2, band], COT[2]) + nt(WB[3, band], COT[3])
-        PART[band] = acc.astype(BF16)
-        r_part.append(send(PART.at[band], PARTR.at[band], "cfg"))
-
     r_k[3].wait_recv()
     r_v[3].wait_recv()
     for h in range(NH):
@@ -229,20 +235,6 @@
         DOT[0, RANK + h * HD:RANK + (h + 1) * HD] = (base + tn(LOW[:, hs], DOT[0, :RANK])).astype(BF16)
         r_do.append({4 - d: send(DOT.at[0, band], DOT.at[4 - d, band], "z%d" % d) for d in (1, 3)})
 
-    forward(2, 1)
-    forward(1, 1)
-    send_do(0)
-    forward(3, 1)
-    send_do(1)
-    forward(0, 1)
-    STO[4 * NH:] = jnp.zeros((16 - 4 * NH, T), F32)
-    r_st = ring("z", lambda d: STO, lambda e: STR.at[e - 1])
-    send_do(2)
-    for h in range(NH):
-        KT[h] = K[:, h * HD:(h + 1) * HD].T
-
-    r_dl = []
-
     def relay_do(h):
         lo, n = bands[h].start, bands[h].stop - bands[h].start
         one = pl.ds(lo, n // 2)
@@ -253,6 +245,21 @@
         b = send(DOT.at[1, two], DOT.at[2, two], "z3")
         r_do[h][2] = [a, b]
 
+    forward(2, 1)
+    forward(1, 1)
+    send_do(0)
+    forward(3, 1)
+    send_do(1)
+    forward(0, 1)
+    STO[4 * NH:] = jnp.zeros((16 - 4 * NH, T), F32)
+    r_st = ring("z", lambda d: STO, lambda e: STR.at[e - 1])
+    relay_do(0)
+    send_do(2)
+    for h in range(NH):
+        KT[h] = K[:, h * HD:(h + 1) * HD].T
+
+    r_dl = []
+
     def send_delta(h):
         for d in (0, 1, 3, 2):
             if d == 2:
@@ -263,7 +270,8 @@
         DLO[h, 4:] = jnp.zeros((4, T), F32)
         r_dl.append(ring("z", lambda d: DLO.at[h], lambda e: DLR.at[h, e - 1]))
 
-    relay_do(0)
+    send_delta(0)
+    relay_do(1)
     for e in (1, 3, 2):
         r_st[e].wait_recv()
     fac, share = {}, {}
@@ -286,11 +294,9 @@
                     lhz += LHR[e - 1, h * RANK:(h + 1) * RANK].astype(F32) * share[h, 0][e]
             lhz = lhz * coef
             LHY[...] = lhz.astype(BF16)
-            names = ("y1", "y3", "y2", "cfg", "cy1", "cy3", "cy2")
-            r_lhy = [send(LHY, LHYR.at[i], to) for i, to in enumerate(names)]
-    relay_do(1)
-    send_delta(0)
+            r_lhy = send(LHY, LHYR, "cfg")
     relay_do(2)
+    send_delta(1)
     slope = [jnp.zeros((RANK, HD), F32) for _ in range(NH)]
     for d in (0, 1, 3, 2):
         for h in range(NH):
@@ -315,7 +321,7 @@
         dp = nn(V[ks, hs], do)
         p = PR[h, ks, qs].astype(F32) * fac[h, d][half]
         ds = (p * (dp - delta[h, d])).astype(BF16)
-        dk = nn(ds, Q[qs, hs]) * SCALE
+        dk = nn(ds, Q[qs, hs])
         dv = nt(p.astype(BF16), do)
         dq = nn(KT[h, :, ks], ds) * SCALE
         if half == 1:
@@ -331,6 +337,7 @@
 
     def half_done(h, half, dk, dv):
         ks = slice(half * NK // 2, (half + 1) * NK // 2)
+        dk = dk * SCALE
         DK[h, ks] = dk
         DV[h, ks] = dv
         r = 1 + 2 * half
@@ -366,39 +373,48 @@
     chain = {}
 
     def chain_gup():
-        lhs = lhz
-        for i, cp in enumerate(r_lhy):
-            cp.wait_recv()
-            lhs += LHYR[i].astype(F32)
-        gup = nn(lhs.astype(BF16), COT[0])
-        for t in range(16):
-            GSB[t, 0:4] = gup[t * 4:(t + 1) * 4]
-            for h in range(NH):
-                GSB[t, 4:8, h * HD:(h + 1) * HD] = slope[h][t * 4:(t + 1) * 4]
+        r_lhy.wait_recv()
+        lhs = (lhz + LHYR[...].astype(F32)).astype(BF16)
+        for j in range(4):
+            gup = nn(lhs, COT[j]).astype(BF16)
+            for t in range(4):
+                GSB[t, j, 0:16] = gup[t * 16:(t + 1) * 16]
+        for h in range(NH):
+            for t in range(4):
+                GSB[t, 0, 16:32, h * HD:(h + 1) * HD] = slope[h][t * 16:(t + 1) * 16].astype(BF16)
         chain["gs"] = []
-        for d in (1, 3, 2, 0):
-            for r in range(4):
-                if r or d:
-                    i = ((4 - d) % 4) * 4 + r
-                    to = ((z + d) % 4) * 4 + px[r] * 2 + pk[r]
-                    chain["gs"].append(send(GSB.at[to], GSR.at[i], "s%d%d" % (d, r)))
+        for t in (1, 3, 2, 0):
+            for d in (1, 3, 2, 0):
+                if t or d:
+                    to = "yz%d%d" % (d, t) if t and d else "z%d" % t if t else "y%d" % d
+                    rows = pl.ds(0, 16 if d else 32)
+                    src = GSB.at[(z + t) % 4, d, rows]
+                    chain["gs"].append(send(src, GSR.at[(4 - t) % 4, (4 - d) % 4, rows], to))
 
     def chain_plane():
         for cp in chain["gs"]:
             cp.wait_recv()
-        s1 = GSB[s]
-        for i in range(1, 16):
-            s1 += GSR[i]
-        S1[c, g] = s1
+        gu = GSB[z, 0, 0:16].astype(F32)
+        sl = GSB[z, 0, 16:32].astype(F32)
+        for t in range(4):
+            for d in range(4):
+                if t or d:
+                    gu += GSR[t, d, 0:16].astype(F32)
+            if t:
+                sl += GSR[t, 0, 16:32].astype(F32)
+        S1[c, g, 0:16] = gu.astype(BF16)
+        S1[c, g, 16:32] = sl.astype(BF16)
         names = ("sib", "x", "xo", "cfg", "c1", "c2", "c3")
         chain["s1"] = [send(S1.at[c, g], S1.at[c, g], to) for to in names]
 
     def chain_yz():
         for cp in chain["s1"]:
             cp.wait_recv()
+        both = []
         for b in range(2):
-            GU[0, 0, b] = jnp.concatenate([S1[b, i, 0:4] for i in range(4)], axis=0).astype(BF16)
-        SL[0] = jnp.concatenate([S1[0, i, 4:8] + S1[1, i, 4:8] for i in range(4)], axis=0).astype(BF16)
+            both.append(S1[b, 0].astype(F32) + S1[b, 1].astype(F32) + S1[b, 2].astype(F32) + S1[b, 3].astype(F32))
+            GU[0, 0, b] = both[b][0:16].astype(BF16)
+        SL[0] = (both[0][16:32] + both[1][16:32]).astype(BF16)
         chain["sl"] = ring("z", lambda d: SL.at[0], lambda e: SL.at[e])
         chain["gu"] = ring("y", lambda d: GU.at[0, 0], lambda e: GU.at[0, e])
         chain["guz"] = ring("z", lambda d: GU.at[0, 0], lambda e: GU.at[e, 0])
@@ -421,16 +437,16 @@
                     col = pl.multiple_of((((hy + j) % 4) * 2 + b) * W, 128)
                     gup_out[rows, pl.ds(col, W)] = GU[d, j, b].astype(F32)
 
+    chain_gup()
     get_delta(0)
     hooks = {
-        (0, 1, 1): [lambda: send_delta(1), chain_gup],
-        (0, 1, 3): [lambda: send_delta(2)],
+        (0, 1, 1): [lambda: send_delta(2)],
         (0, 0, 1): [lambda: cross(0)],
         (0, 0, 3): [lambda: get_delta(1)],
         (1, 1, 3): [chain_plane],
         (1, 0, 1): [lambda: cross(1)],
         (1, 0, 3): [lambda: get_delta(2)],
-        (2, 1, 3): [chain_yz],
+        (2, 0, 0): [chain_yz],
         (2, 0, 1): [lambda: cross(2)],
     }
     for h in range(NH):
@@ -453,9 +469,18 @@
 
 
 def hand_over(*refs):
-    n = len(refs) // 2
-    for i in range(n):
-        refs[n + i][...] = refs[i][...]
+    n = len(refs) // 3
+    sems = refs[-1]
+    reads = [pltpu.make_async_copy(refs[i], refs[2 * n + i], sems.at[i]) for i in range(n)]
+    writes = [pltpu.make_async_copy(refs[2 * n + i], refs[n + i], sems.at[n + i]) for i in range(n)]
+    order = (4, 0, 1, 2, 3)
+    for i in order:
+        reads[i].start()
+    for i in order:
+        reads[i].wait()
+        writes[i].start()
+    for i in order:
+        writes[i].wait()
 
 
 def scratch():
@@ -496,10 +521,10 @@
         v((3, NH * RANK, T), BF16),
         v((NH, RANK, T), F32),
         v((RANK, T), BF16),
-        v((7, RANK, T), BF16),
-        v((16, 8, W), F32),
-        v((16, 8, W), F32),
-        v((2, 4, 8, W), F32),
+        v((RANK, T), BF16),
+        v((4, 4, 32, W), BF16),
+        v((4, 4, 32, W), BF16),
+        v((2, 4, 32, W), BF16),
         v((4, 4, 2, 16, W), BF16),
         v((4, 16, W), BF16),
         pltpu.SemaphoreType.DMA((NSEM,)),
@@ -533,8 +558,9 @@
     dq, dk, dv, slope, gup = pl.pallas_call(
         hand_over,
         out_shape=shapes,
-        in_specs=[vmem] * 5,
-        out_specs=(vmem,) * 5,
+        in_specs=[hbm] * 5,
+        out_specs=(hbm,) * 5,
+        scratch_shapes=[pltpu.VMEM(a.shape, a.dtype) for a in shapes] + [pltpu.SemaphoreType.DMA((10,))],
         cost_estimate=pl.CostEstimate(flops=0, bytes_accessed=4 * 10**6, transcendentals=0),
     )(*parts)
     return dq[None], dk[None], dv[None], slope.T, gup

time: 71.3 us -> 69 us (0.968)
  Pallas kernels: 69.4 us -> 67.1 us
    pallas_call x1, Pallas kernels: 66.8 us -> 64.8 us  [per_device(): pl.pallas_call(kernel, out_shape=shapes, in_specs=[hbm] * 7 + [smem] * 3,...]
where the time goes in v4:
time: 69 us; the launch traced here: 68.6 us
  Pallas kernels  67.1 us (97%)
  between operations  1.45 us (2%)
    pallas_call x1, Pallas kernels, per_device(): pl.pallas_call(kernel, out_shape=shapes, in_specs=[hbm] * 7 + [smem] * 3,...  64.8 us
    pallas_call x1, Pallas kernels, per_device(): pl.pallas_call(hand_over, out_shape=shapes, in_specs=[hbm] * 5, out_specs...  2.31 us

profile of v4, /device:TPU:0, one launch (start us, length us, event | category | flops | bytes accessed | tf_op | source)
XLA Modules:
  0.0 68.6 jit_solution(3660398066872879803)
XLA Ops:
  1.3 64.8 %shard_map.137 = (bf16[256,384]{1,0:T(8,128)(2,1)}, bf16[256,384]{1,0:T(8,128)(2,1)}, bf16[256,384]{1,0:T(8,128)(2,1)}, f32[64,384]{1,0:T(8,128)}, f32[64,3072]{1,0:T(8,128)}) custom-call(bf16[256,384]{1,0:T(8,128)(2,1)} %bitcast.8, bf16[256,384]{1,0:T(8,128)(2,1)} %bitcast.9, bf16[256,384]{1,0:T(8,128)(2,1)} %bitcast.10, bf16[256,384]{1,0:T(8,128)(2,1)} %cot_in.1, ...), custom_call_target="tpu_custom_call" | custom-call | flops 10000000000 | bytes 8000000 | tf_op jit(solution)/shard_map/pallas_call | solution.py:547
  66.1 2.3 %shard_map.138 = (bf16[256,384]{1,0:T(8,128)(2,1)}, bf16[256,384]{1,0:T(8,128)(2,1)}, bf16[256,384]{1,0:T(8,128)(2,1)}, f32[64,384]{1,0:T(8,128)}, f32[64,3072]{1,0:T(8,128)}) custom-call(bf16[256,384]{1,0:T(8,128)(2,1)} %get-tuple-element.15.refs_0_, bf16[256,384]{1,0:T(8,128)(2,1)} %get-tuple-element.16.refs_1_, ...), custom_call_target="tpu_custom_call" | custom-call | bytes 4000000 | tf_op jit(solution)/shard_map/pallas_call | solution.py:558

commit v5 on v4

--- a/solution.py
+++ b/solution.py
@@ -246,15 +246,16 @@
         r_do[h][2] = [a, b]
 
     forward(2, 1)
+    send_do(0)
     forward(1, 1)
-    send_do(0)
+    send_do(1)
     forward(3, 1)
-    send_do(1)
+    send_do(2)
     forward(0, 1)
     STO[4 * NH:] = jnp.zeros((16 - 4 * NH, T), F32)
     r_st = ring("z", lambda d: STO, lambda e: STR.at[e - 1])
     relay_do(0)
-    send_do(2)
+    relay_do(1)
     for h in range(NH):
         KT[h] = K[:, h * HD:(h + 1) * HD].T
 
@@ -270,8 +271,7 @@
         DLO[h, 4:] = jnp.zeros((4, T), F32)
         r_dl.append(ring("z", lambda d: DLO.at[h], lambda e: DLR.at[h, e - 1]))
 
-    send_delta(0)
-    relay_do(1)
+    relay_do(2)
     for e in (1, 3, 2):
         r_st[e].wait_recv()
     fac, share = {}, {}
@@ -295,8 +295,9 @@
             lhz = lhz * coef
             LHY[...] = lhz.astype(BF16)
             r_lhy = send(LHY, LHYR, "cfg")
-    relay_do(2)
+    send_delta(0)
     send_delta(1)
+    send_delta(2)
     slope = [jnp.zeros((RANK, HD), F32) for _ in range(NH)]
     for d in (0, 1, 3, 2):
         for h in range(NH):
@@ -440,7 +441,6 @@
     chain_gup()
     get_delta(0)
     hooks = {
-        (0, 1, 1): [lambda: send_delta(2)],
         (0, 0, 1): [lambda: cross(0)],
         (0, 0, 3): [lambda: get_delta(1)],
         (1, 1, 3): [chain_plane],

time: 69 us -> 68.5 us (level)
  Pallas kernels: 67.1 us -> 66.4 us
    pallas_call x1, Pallas kernels: 64.8 us -> 64.1 us  [per_device(): pl.pallas_call(kernel, out_shape=shapes, in_specs=[hbm] * 7 + [smem] * 3,...]
where the time goes in v5:
time: 68.5 us; the launch traced here: 67.9 us
  Pallas kernels  66.4 us (97%)
  between operations  1.45 us (2%)
    pallas_call x1, Pallas kernels, per_device(): pl.pallas_call(kernel, out_shape=shapes, in_specs=[hbm] * 7 + [smem] * 3,...  64.1 us
    pallas_call x1, Pallas kernels, per_device(): pl.pallas_call(hand_over, out_shape=shapes, in_specs=[hbm] * 5, out_specs...  2.31 us

profile of v5, /device:TPU:0, one launch (start us, length us, event | category | flops | bytes accessed | tf_op | source)
XLA Modules:
  0.0 67.9 jit_solution(7899831775588039790)
XLA Ops:
  1.3 64.1 %shard_map.137 = (bf16[256,384]{1,0:T(8,128)(2,1)}, bf16[256,384]{1,0:T(8,128)(2,1)}, bf16[256,384]{1,0:T(8,128)(2,1)}, f32[64,384]{1,0:T(8,128)}, f32[64,3072]{1,0:T(8,128)}) custom-call(bf16[256,384]{1,0:T(8,128)(2,1)} %bitcast.8, bf16[256,384]{1,0:T(8,128)(2,1)} %bitcast.9, bf16[256,384]{1,0:T(8,128)(2,1)} %bitcast.10, bf16[256,384]{1,0:T(8,128)(2,1)} %cot_in.1, ...), custom_call_target="tpu_custom_call" | custom-call | flops 10000000000 | bytes 8000000 | tf_op jit(solution)/shard_map/pallas_call | solution.py:547
  65.4 2.3 %shard_map.138 = (bf16[256,384]{1,0:T(8,128)(2,1)}, bf16[256,384]{1,0:T(8,128)(2,1)}, bf16[256,384]{1,0:T(8,128)(2,1)}, f32[64,384]{1,0:T(8,128)}, f32[64,3072]{1,0:T(8,128)}) custom-call(bf16[256,384]{1,0:T(8,128)(2,1)} %get-tuple-element.15.refs_0_, bf16[256,384]{1,0:T(8,128)(2,1)} %get-tuple-element.16.refs_1_, ...), custom_call_target="tpu_custom_call" | custom-call | bytes 4000000 | tf_op jit(solution)/shard_map/pallas_call | solution.py:558
